TPU v7x, 128 devices: a whole 4x4x4 slice. The times are simulated.
128 devices in a mesh: dp: 32 (over x, y, core), seq: 4 (over z).
Axes of the slice: x: 4, y: 4, z: 4, core: 2. Of those that a mesh axis runs over, the one named last changes fastest.
Arguments:
- inputs: bfloat16 [2, 32, 512, 1024], P(None, 'dp', 'seq'), may hold values from -6 to 6
- starts: int32 [2, 32, 512], P(None, 'dp', 'seq'), may hold values from 0 to 511, as said below
- w_query: bfloat16 [1024, 1024], P('dp'), may hold values from -0.1875 to 0.1875
- key_weight: bfloat16 [1024, 512], P('dp'), may hold values from -0.1875 to 0.1875
- value_weight: bfloat16 [1024, 512], P('dp'), may hold values from -0.1875 to 0.1875
- w_out: bfloat16 [1024, 1024], P('dp'), may hold values from -0.75 to 0.75
- w_gate: bfloat16 [1024, 4608], P('dp'), may hold values from -0.1875 to 0.1875
- w_up: bfloat16 [1024, 4608], P('dp'), may hold values from -0.1875 to 0.1875
- w_down: bfloat16 [4608, 1024], P('dp'), may hold values from -0.09375 to 0.09375
- prenorm: bfloat16 [1024], P('dp'), may hold values from 0.5 to 1.5
- midnorm: bfloat16 [1024], P('dp'), may hold values from 0.5 to 1.5
- querynorm: bfloat16 [64], P('dp'), may hold values from 1 to 2
- keynorm: bfloat16 [64], P('dp'), may hold values from 1 to 2
- cotangent: bfloat16 [2, 32, 512, 1024], P(None, 'dp', 'seq'), may hold values from -6 to 6
Outputs:
- outputs: bfloat16 [2, 32, 512, 1024], P(None, 'dp', 'seq')
- grad_inputs: float32 [2, 32, 512, 1024], P(None, 'dp', 'seq')
- dw_query: float32 [1024, 1024], P('dp')
- dw_key: float32 [1024, 512], P('dp')
- dw_value: float32 [1024, 512], P('dp')
- dw_out: float32 [1024, 1024], P('dp')
- dw_gate: float32 [1024, 4608], P('dp')
- dw_up: float32 [1024, 4608], P('dp')
- dw_down: float32 [4608, 1024], P('dp')
- grad_prenorm: float32 [1024], P('dp')
- grad_midnorm: float32 [1024], P('dp')
- grad_querynorm: float32 [64], P('dp')
- grad_keynorm: float32 [64], P('dp')
Inputs may be any that keep to these rules, and one draw needn't show every extreme that they name: Documents are contiguous: in each row a value is the first position that holds it and values never fall. One document of each row starts before position 64 and covers position 448; at most one short document precedes it and one short document follows it, ending the row.
All inputs are finite; a program needn't handle non-finite values.
Results may differ from a plain program's by a relative error of at most 0.04.
Values may be sent and summed in bfloat16 or wider, within the bound.
A program may use at most 192 MiB of HBM per device.

v0:
```python
from functools import partial

import jax
import jax.numpy as jnp
from jax import lax
from jax.experimental import pallas as pl
from jax.experimental.pallas import tpu as pltpu
from jax.sharding import PartitionSpec as P

QUERY_HEADS = 16
KEY_VALUE_HEADS = 8
HEAD_SIZE = 64
EPS = 1e-05
ROPE_BASE = 1000000.0

MESH = pl.DeviceIdType.MESH
BF = jnp.bfloat16
F32 = jnp.float32
WA = 3200
GU = 2304
DN = 144


class Links:
    def __init__(self, send, recv, local):
        dp = lax.axis_index("dp")
        self.z = lax.axis_index("seq")
        self.x, self.y, self.c = dp // 8, (dp // 2) % 4, dp % 2
        self.send, self.recv, self.local = send, recv, local
        self.n = self.m = 0
        self.out = []
        self.other = 1 - self.c
        place = {"x": self.x, "y": self.y, "z": self.z}
        self.ring = {k: ((v + 3) % 4, (v + 1) % 4, (v + 2) % 4) for k, v in place.items()}
        self.past_x = (self.x - self.z + 4) % 4
        self.past_z = (self.z - self.x + 4) % 4
        self.near = {("c", 1): self.dev(self.x, self.y, self.other, self.z)}
        for k, (before, after, far) in self.ring.items():
            for step, v in ((-1, before), (1, after)):
                spot = dict(place, **{k: v})
                self.near[k, step] = self.dev(spot["x"], spot["y"], self.c, spot["z"])

    def dev(self, x, y, c, z):
        return ((x * 4 + y) * 2 + c, z)

    def nbr(self, axis, step):
        return self.near[axis, step]

    def sides(self, axis):
        return self.nbr(axis, 1), self.nbr(axis, -1)

    def barrier(self, axes):
        sem = pltpu.get_barrier_semaphore()
        count = 0
        for axis in axes:
            for step in (1,) if axis == "c" else (1, -1):
                pl.semaphore_signal(sem, inc=1, device_id=self.nbr(axis, step), device_id_type=MESH)
                count += 1
        pl.semaphore_wait(sem, count)

    def make(self, src, dst, to):
        copy = pltpu.make_async_remote_copy(
            src_ref=src,
            dst_ref=dst,
            send_sem=self.send.at[self.n],
            recv_sem=self.recv.at[self.n],
            device_id=to,
            device_id_type=MESH,
        )
        self.n += 1
        return copy

    def put(self, src, dst, to):
        copy = self.make(src, dst, to)
        copy.start()
        self.out.append(copy)
        return copy

    def keep(self, src, dst):
        copy = pltpu.make_async_copy(src, dst, self.local.at[self.m])
        self.m += 1
        copy.start()
        return copy

    def flush(self):
        for copy in self.out:
            copy.wait_send()
        self.out = []


def drive(*steps):
    steps = list(steps)
    while steps:
        steps = [s for s in steps if next(s, "end") != "end"]


def ring_gather(lk, own, slot, part, axis, me, ready=None):
    right, left = lk.sides(axis)
    before, after, far = lk.ring[axis]
    a = lk.put(own, slot(me), right)
    b = lk.put(own, slot(me), left)
    yield 1
    a.wait_recv()
    c = lk.put(part(before, 0), part(before, 0), right)
    if ready:
        ready(before)
    b.wait_recv()
    d = lk.put(part(after, 1), part(after, 1), left)
    if ready:
        ready(after)
    yield 1
    c.wait_recv()
    d.wait_recv()
    if ready:
        ready(far)


def plane_gather(lk, own, out, first, lo, hi):
    cols = pl.ds(lo, hi - lo)
    x, y, c = lk.x, lk.y, lk.c
    kept = lk.keep(own.at[:, cols], out.at[x, y, c, :, cols])
    crossing = []

    def cross(ref):
        crossing.append(lk.put(ref, ref, lk.nbr("c", 1)))

    def rows(k):
        return pl.ds(16 * k, 16)

    def two(k):
        return pl.ds(2 * k, 2)

    if first == "x":
        yield from ring_gather(
            lk, own.at[:, cols], lambda i: out.at[i, y, c, :, cols],
            lambda i, k: out.at[i, y, c, rows(k), cols], "x", x,
        )
        kept.wait()
        whole = out.at[:, y, c, :, cols]
        cross(whole)
        yield from ring_gather(
            lk, whole, lambda j: out.at[:, j, c, :, cols],
            lambda j, k: out.at[two(k), j, c, :, cols], "y", y,
            lambda j: cross(out.at[:, j, c, :, cols]),
        )
    else:
        yield from ring_gather(
            lk, own.at[:, cols], lambda j: out.at[x, j, c, :, cols],
            lambda j, k: out.at[x, j, c, rows(k), cols], "y", y,
        )
        kept.wait()
        whole = out.at[x, :, c, :, cols]
        cross(whole)
        yield from ring_gather(
            lk, whole, lambda i: out.at[i, :, c, :, cols],
            lambda i, k: out.at[i, two(k), c, :, cols], "x", x,
            lambda i: cross(out.at[i, :, c, :, cols]),
        )
    yield 1
    for copy in crossing:
        copy.wait_recv()


def ring_spread(lk, own, dst, part, axis, place):
    right, left = lk.sides(axis)
    a, b = lk.make(own, dst, right), lk.make(own, dst, left)
    c, d = lk.make(part(0), part(0), right), lk.make(part(1), part(1), left)
    kept = pltpu.make_async_copy(own, dst, lk.local.at[lk.m])
    lk.m += 1

    @pl.when(place == 0)
    def _():
        a.start()
        b.start()
        kept.start()

    yield 1

    @pl.when(place == 1)
    def _():
        a.wait_recv()
        c.start()

    @pl.when(place == 3)
    def _():
        b.wait_recv()
        d.start()

    yield 1

    @pl.when(place == 2)
    def _():
        c.wait_recv()
        d.wait_recv()

    @pl.when(place == 0)
    def _():
        kept.wait()
        a.wait_send()
        b.wait_send()

    @pl.when(place == 1)
    def _():
        c.wait_send()

    @pl.when(place == 3)
    def _():
        d.wait_send()


def down_part(k):
    return pl.ds(0, 80) if k == 0 else pl.ds(80, 64)


def down_gather(lk, own, out):
    y, c = lk.y, lk.c
    yield from ring_spread(
        lk, own, out.at[y, c], lambda k: out.at[y, c, down_part(k)], "x", lk.past_x
    )
    crossing = []

    def cross(j):
        crossing.append(lk.put(out.at[j, c], out.at[j, c], lk.nbr("c", 1)))

    cross(y)
    yield from ring_gather(
        lk, out.at[y, c], lambda j: out.at[j, c], lambda j, k: out.at[j, c, down_part(k)], "y", y, cross
    )
    yield 1
    for copy in crossing:
        copy.wait_recv()


def line_gather(lk, own, out, cut):
    z, rows = lk.z, own.shape[0]
    kept = lk.keep(own, out.at[z])

    def part(i, k):
        return out.at[i, pl.ds(0, cut)] if k == 0 else out.at[i, pl.ds(cut, rows - cut)]

    yield from ring_gather(lk, own, lambda i: out.at[i], part, "z", z)
    kept.wait()


def add_into(dst, src):
    if len(dst.shape) == 2:
        dst[...] = (dst[...].astype(F32) + src[...].astype(F32)).astype(BF)
    else:
        for i in range(dst.shape[0]):
            dst[i] = (dst[i].astype(F32) + src[i].astype(F32)).astype(BF)


def ring_reduce(lk, p, part, bufs, axis, me):
    right, left = lk.sides(axis)
    r0, r1, ra, rb = bufs
    before, after, far = lk.ring[axis]
    a = lk.put(part(far, 0), r0, right)
    b = lk.put(part(far, 1), r1, left)
    yield 1
    a.wait_recv()
    add_into(part(after, 0), r0)
    c = lk.put(p(after), ra, right)
    b.wait_recv()
    add_into(part(before, 1), r1)
    d = lk.put(p(before), rb, left)
    yield 1
    c.wait_recv()
    add_into(p(me), ra)
    d.wait_recv()
    add_into(p(me), rb)


def plane_reduce(lk, spot, sib_src, sib, bufs, out, first, kept=None):
    x, y, c = lk.x, lk.y, lk.c
    one, two = bufs
    got = lk.put(sib_src, sib, lk.nbr("c", 1))
    yield 1
    if kept is not None:
        kept.wait()
    got.wait_recv()

    def step(i, _):
        ref = spot(i // 4, i % 4)
        ref[...] = (ref[...].astype(F32) + sib[i // 4, i % 4].astype(F32)).astype(BF)
        return 0

    lax.fori_loop(0, 16, step, 0)
    every = slice(None)

    def pair(k):
        return pl.ds(2 * k, 2)

    def rows(ref, k):
        return ref.at[pl.ds(16 * k, 16)]

    if first == "y":
        yield from ring_reduce(lk, lambda j: spot(every, j), lambda j, k: spot(pair(k), j), one, "y", y)
        yield from ring_reduce(lk, lambda i: spot(i, y), lambda i, k: rows(spot(i, y), k), two, "x", x)
    else:
        yield from ring_reduce(lk, lambda i: spot(i, every), lambda i, k: spot(i, pair(k)), one, "x", x)
        yield from ring_reduce(lk, lambda j: spot(x, j), lambda j, k: rows(spot(x, j), k), two, "y", y)
    done = lk.keep(spot(x, y), out)
    yield 1
    done.wait()


def ring_scratch(cols):
    return [
        pltpu.VMEM((4, 4, 32, cols), BF),
        pltpu.VMEM((2, 32, cols), BF),
        pltpu.VMEM((2, 32, cols), BF),
        pltpu.VMEM((4, 32, cols), BF),
        pltpu.VMEM((4, 32, cols), BF),
        pltpu.VMEM((16, cols), BF),
        pltpu.VMEM((16, cols), BF),
        pltpu.VMEM((32, cols), BF),
        pltpu.VMEM((32, cols), BF),
    ]


def down_scratch():
    return [
        pltpu.VMEM((4, DN, 1024), BF),
        pltpu.VMEM((4, DN, 1024), BF),
        pltpu.VMEM((80, 1024), BF),
        pltpu.VMEM((64, 1024), BF),
        pltpu.VMEM((DN, 1024), BF),
        pltpu.VMEM((DN, 1024), BF),
        pltpu.VMEM((80, 1024), BF),
        pltpu.VMEM((64, 1024), BF),
        pltpu.VMEM((DN, 1024), BF),
        pltpu.VMEM((DN, 1024), BF),
    ]


def down_reduce(lk, part_hbm, s, out):
    acc, sib, one, (x0, x1, xa, xb) = s[0], s[1], s[2:6], s[6:10]
    y, c = lk.y, lk.c
    kept = lk.keep(part_hbm.at[:, c], acc)
    got = lk.put(part_hbm.at[:, 1 - c], sib, lk.nbr("c", 1))
    yield 1
    kept.wait()
    got.wait_recv()
    add_into(acc, sib)
    yield from ring_reduce(
        lk, lambda j: acc.at[j], lambda j, k: acc.at[j, down_part(k)], one, "y", y
    )
    mine = acc.at[y]
    right, left = lk.sides("x")
    place = lk.past_x
    a = lk.make(acc.at[y, down_part(0)], x0, left)
    b = lk.make(acc.at[y, down_part(1)], x1, right)
    e = lk.make(mine, xa, left)
    f = lk.make(mine, xb, right)

    @pl.when(place == 2)
    def _():
        a.start()
        b.start()

    yield 1

    @pl.when(place == 1)
    def _():
        a.wait_recv()
        add_into(acc.at[y, down_part(0)], x0)
        e.start()

    @pl.when(place == 3)
    def _():
        b.wait_recv()
        add_into(acc.at[y, down_part(1)], x1)
        f.start()

    yield 1

    @pl.when(place == 0)
    def _():
        e.wait_recv()
        add_into(mine, xa)
        f.wait_recv()
        add_into(mine, xb)

    @pl.when(place == 1)
    def _():
        e.wait_send()

    @pl.when(place == 3)
    def _():
        f.wait_send()

    @pl.when(place == 2)
    def _():
        a.wait_send()
        b.wait_send()

    yield from ring_spread(
        lk, mine, out, lambda k: out.at[down_part(k)], "z", lk.past_z
    )


ANY = pl.BlockSpec(memory_space=pl.ANY)


def sems(n):
    return [pltpu.SemaphoreType.DMA((n,)), pltpu.SemaphoreType.DMA((n,)), pltpu.SemaphoreType.DMA((40,))]


def params(number):
    return pltpu.CompilerParams(collective_id=number, has_side_effects=True, vmem_limit_bytes=56 * 2**20)


def shape(*dims, dtype=BF):
    return jax.ShapeDtypeStruct(dims, dtype)


def lanes_of(shape):
    return lax.broadcasted_iota(jnp.int32, shape, len(shape) - 1)


def dot(left, right, dims=((1,), (0,)), kind=F32):
    return lax.dot_general(left, right, (dims, ((), ())), preferred_element_type=F32).astype(kind)


TOKENS = ((0,), (0,))
ROWS = ((1,), (1,))


def flat(value):
    return value.reshape(-1, value.shape[-1])


def head_ones():
    row = lax.broadcasted_iota(jnp.int32, (256, 256), 0) // 64
    col = lax.broadcasted_iota(jnp.int32, (256, 256), 1) // 64
    return jnp.where(row == col, 1.0 / 64, 0.0).astype(BF)


def head_mean(v, ones):
    high = v.astype(BF)
    low = (v - high.astype(F32)).astype(BF)
    return dot(high, ones) + dot(low, ones)


def halves_swapped(v):
    lane = lanes_of(v.shape)
    return jnp.where(lane % 64 < 32, pltpu.roll(v, 96, 1), pltpu.roll(v, 32, 1))


def angle_tables(tab):
    lane = lanes_of(tab.shape)
    other = pltpu.roll(tab, 64, 1)
    return jnp.where(lane < 64, tab, other), jnp.where(lane < 64, other, tab)


def row_scale(v):
    return lax.rsqrt(jnp.mean(v * v, axis=-1, keepdims=True) + EPS)


def gain_rows(whole, gain):
    def step(i, total):
        return total + whole[i // 8, (i // 2) % 4, i % 2, :, pl.ds(2048, 128)].astype(F32)

    total = lax.fori_loop(0, 32, step, jnp.zeros((32, 128), F32))
    for k in range(8):
        gain[0:1, pl.ds(128 * k, 128)] = total[8 + k : 9 + k]
        gain[1:2, pl.ds(128 * k, 128)] = total[16 + k : 17 + k]
        gain[2:3, pl.ds(128 * k, 128)] = total[0:1]
        gain[3:4, pl.ds(128 * k, 128)] = total[1:2]


def keys_values(whole, sources, tables, gain, normed, keys, values, lin_key, own):
    ones = head_ones()

    def step(q, _):
        src = sources[q].astype(F32)
        normed[q] = (src * row_scale(src) * gain[0:1]).astype(BF)
        cosine, sine = angle_tables(tables[q])
        kn = gain[3:4, 0:128]
        lane = lanes_of((256, 128))

        def put(ref, tile, r):
            turned = pltpu.roll(r, 64, 1)
            even = jnp.where(lane < 64, r, turned).astype(BF)
            odd = jnp.where(lane < 64, turned, r).astype(BF)
            for m in range(2):
                ref[m, 2 * tile, pl.ds(q * 128, 128)] = even[128 * m : 128 * m + 128]
                ref[m, 2 * tile + 1, pl.ds(q * 128, 128)] = odd[128 * m : 128 * m + 128]

        for j in range(4):
            lin = dot(normed[q], flat(whole[:, :, :, :, pl.ds(1024 + 256 * j, 256)]))
            if j < 2:
                scale = lax.rsqrt(head_mean(lin * lin, ones) + EPS)

                @pl.when(q == own)
                def _():
                    lin_key[:, pl.ds(256 * j, 256)] = lin

                for h in range(2):
                    cut = slice(128 * h, 128 * h + 128)
                    v = lin[:, cut] * scale[:, cut] * kn
                    put(keys, 2 * j + h, v * cosine + halves_swapped(v) * sine)
            else:
                for h in range(2):
                    put(values, 2 * (j - 2) + h, lin[:, 128 * h : 128 * h + 128])
        return 0

    lax.fori_loop(0, 4, step, 0)


def own_queries(whole, tables, gain, normed, lin_query, queries, own):
    ones = head_ones()
    cosine, sine = angle_tables(tables[own])
    qn = gain[2:3, 0:128]
    lane = lanes_of((256, 128))

    def step(j, _):
        lin = dot(normed[own], flat(whole[:, :, :, :, pl.ds(pl.multiple_of(256 * j, 256), 256)]))
        lin_query[:, pl.ds(pl.multiple_of(256 * j, 256), 256)] = lin
        scale = lax.rsqrt(head_mean(lin * lin, ones) + EPS)
        for h in range(2):
            cut = slice(128 * h, 128 * h + 128)
            v = lin[:, cut] * scale[:, cut] * qn
            r = (v * cosine + halves_swapped(v) * sine) * HEAD_SIZE ** (-0.5)
            first = jnp.where(lane < 64, r, 0.0).astype(BF)
            second = jnp.where(lane < 64, 0.0, r).astype(BF)
            for m in range(2):
                queries[m, 2 * j + h, 0:128] = first[128 * m : 128 * m + 128]
                queries[m, 2 * j + h, 128:256] = second[128 * m : 128 * m + 128]
        return 0

    lax.fori_loop(0, 4, step, 0)


def attend(queries, keys, values, starts, probs, mixed, own):
    key_pos = lax.broadcasted_iota(jnp.int32, (512, 256), 0)
    query_pos = own * 128 + lax.broadcasted_iota(jnp.int32, (1, 256), 1) % 128
    lane = lanes_of((128, 128))

    def step(i, _):
        m, k = i // 8, i % 8
        row = starts[pl.ds(m, 1)]
        begin = jnp.concatenate([row, row], axis=1)
        scores = dot(keys[m, k], queries[m, k], ROWS)
        scores = jnp.where((key_pos <= query_pos) & (key_pos >= begin), scores, -1e30)
        raised = jnp.exp(scores - jnp.max(scores, axis=0, keepdims=True))
        chance = (raised * (1.0 / jnp.sum(raised, axis=0, keepdims=True))).astype(BF)
        probs[i] = chance
        got = dot(values[m, k], chance, TOKENS).T
        both = jnp.where(lane < 64, got[0:128], got[128:256]).astype(BF)
        mixed[pl.ds(pl.multiple_of(m * 128, 128), 128), pl.ds(pl.multiple_of(k * 128, 128), 128)] = both
        return 0

    lax.fori_loop(0, 16, step, 0)


def out_project(whole, source, gain, mixed, middle, normed_ffn, own):
    def step(j, _):
        cut = pl.ds(pl.multiple_of(256 * j, 256), 256)
        w = flat(whole[:, :, :, :, pl.ds(pl.multiple_of(2176 + 256 * j, 128), 256)])
        middle[:, cut] = source[:, cut].astype(F32) + dot(mixed[...], w)
        return 0

    lax.fori_loop(0, 4, step, 0)
    mid = middle[...]
    normed_ffn[own] = (mid * row_scale(mid) * gain[1:2]).astype(BF)


def feed_back_in(cots, down, grad_hidden):
    def step(i, _):
        grad_hidden[i] = dot(cots[i], flat(down[...]), ROWS, BF)
        return 0

    lax.fori_loop(0, 4, step, 0)


def feed_chunk(i, ffn, gate_up, down, grad_hidden, hidden, turned, ffn_turned, grad_both, grad_ffn, out_part):
    def step(j, _):
        cut = pl.ds(pl.multiple_of(384 * j, 128), 384)
        cut_up = pl.ds(pl.multiple_of(1152 + 384 * j, 128), 384)
        gated = dot(ffn[i], flat(gate_up[:, :, :, :, cut]))
        upward = dot(ffn[i], flat(gate_up[:, :, :, :, cut_up]))
        sigma = 1.0 / (1.0 + jnp.exp(-gated))
        silu = gated * sigma
        made = (silu * upward).astype(BF)
        hidden[:, cut] = made
        turned[i, cut] = made.T
        back = grad_hidden[i, :, cut].astype(F32)
        grad_both[i, :, cut] = (back * upward * sigma * (1.0 + gated * (1.0 - sigma))).astype(BF)
        grad_both[i, :, cut_up] = (back * silu).astype(BF)
        return 0

    lax.fori_loop(0, 3, step, 0)

    def last(j, _):
        cut = pl.ds(pl.multiple_of(256 * j, 256), 256)
        grad_ffn[i, :, cut] = dot(grad_both[i], flat(gate_up[j]), ROWS, BF)
        out_part[i, :, cut] = dot(hidden[...], flat(down[:, :, :, cut]), kind=BF)
        ffn_turned[i, cut] = ffn[i, :, cut].T
        return 0

    lax.fori_loop(0, 4, last, 0)


def feed_grads(left, right, out, tiles):
    def step(j, _):
        cut = pl.ds(pl.multiple_of(256 * j, 256), 256)
        got = dot(left[0], right[0, :, cut])
        for i in range(1, 4):
            got = got + dot(left[i], right[i, :, cut])
        lead = out.shape[:-1]
        out[(slice(None),) * len(lead) + (cut,)] = got.astype(BF).reshape(*lead, 256)
        return 0

    lax.fori_loop(0, tiles, step, 0)


FWD_SCRATCH = [
    pltpu.VMEM((4, 4, 2, 32, WA), BF),
    pltpu.VMEM((4, 4, 2, 32, GU), BF),
    pltpu.VMEM((4, 2, DN, 1024), BF),
    pltpu.VMEM((4, 256, 1024), BF),
    pltpu.VMEM((4, 256, 128), F32),
    pltpu.VMEM((4, 256, 1024), BF),
    pltpu.VMEM((4, 256, 1024), BF),
    pltpu.VMEM((4, 256, 1024), BF),
    pltpu.VMEM((256, 1024), F32),
    pltpu.VMEM((256, 512), F32),
    pltpu.VMEM((2, 8, 512, 128), BF),
    pltpu.VMEM((2, 8, 512, 128), BF),
    pltpu.VMEM((2, 8, 256, 128), BF),
    pltpu.VMEM((16, 512, 256), BF),
    pltpu.VMEM((256, 1024), BF),
    pltpu.VMEM((256, 1024), F32),
    pltpu.VMEM((8, 1024), F32),
    pltpu.VMEM((4, 256, 1152), BF),
    pltpu.VMEM((256, 1152), BF),
    pltpu.VMEM((4, 1152, 256), BF),
    pltpu.VMEM((4, 1024, 256), BF),
    pltpu.VMEM((4, 256, GU), BF),
    pltpu.VMEM((4, 256, 1024), BF),
    pltpu.VMEM((4, 256, 1024), BF),
    pltpu.VMEM((256, 1024), BF),
    pltpu.VMEM((256, 1024), BF),
    pltpu.VMEM((2, 128, 1024), BF),
    pltpu.VMEM((2, 128, 1024), BF),
    pltpu.VMEM((2, 128), jnp.int32),
]

FWD_OUT = (
    shape(4, 4, 2, 32, WA),
    shape(256, 1024),
    shape(256, 1024, dtype=F32),
    shape(256, 512, dtype=F32),
    shape(2, 8, 512, 128),
    shape(2, 8, 512, 128),
    shape(2, 8, 256, 128),
    shape(16, 512, 256),
    shape(256, 1024),
    shape(256, 1024, dtype=F32),
    shape(8, 1024, dtype=F32),
    shape(4, 4, 2, 32, GU),
    shape(4, 2, DN, 1024),
    shape(4, 256, 1024),
    shape(256, 1024, dtype=F32),
)


def fwd_kernel(wa, gu, dn, x, cot, tab, starts_hbm, *refs):
    outs, refs = refs[: len(FWD_OUT)], refs[len(FWD_OUT) :]
    lk = Links(*refs[:3])
    (
        whole, gate_up, down, sources, tables, cots, ffn, normed, lin_query, lin_key, keys, values, queries,
        probs, mixed, middle, gain, grad_hidden, hidden, turned, ffn_turned, grad_both, grad_ffn, out_part,
        from_right, from_left, passing, from_far, starts,
    ) = refs[3:]
    own = lk.z
    before, after, far = (own + 3) % 4, (own + 1) % 4, (own + 2) % 4
    lk.barrier("xyzc")
    first = [
        plane_gather(lk, wa, whole, "x", 0, 1536),
        plane_gather(lk, wa, whole, "y", 1536, WA),
        line_gather(lk, tab, tables, 128),
        line_gather(lk, x, sources, 128),
    ]
    later = [
        plane_gather(lk, gu, gate_up, "x", 0, 1152),
        plane_gather(lk, gu, gate_up, "y", 1152, GU),
        down_gather(lk, dn, down),
        line_gather(lk, cot, cots, 128),
    ]
    for s in first + later[:3]:
        next(s)
    saved = [lk.keep(starts_hbm, starts)]
    saved[0].wait()
    saved = []
    drive(*first)

    def tick():
        for s in later:
            next(s, None)

    tick()
    gain_rows(whole, gain)
    saved.append(lk.keep(whole, outs[0]))
    keys_values(whole, sources, tables, gain, normed, keys, values, lin_key, own)
    tick()
    own_queries(whole, tables, gain, normed, lin_query, queries, own)
    for k, ref in enumerate((normed.at[own], lin_query, lin_key, keys, values, queries)):
        saved.append(lk.keep(ref, outs[1 + k]))
    tick()
    attend(queries, keys, values, starts, probs, mixed, own)
    tick()
    out_project(whole, sources.at[own], gain, mixed, middle, ffn, own)
    for k, ref in enumerate((probs, mixed, middle, gain)):
        saved.append(lk.keep(ref, outs[7 + k]))
    passed = ring_gather(
        lk, ffn.at[own], lambda i: ffn.at[i], lambda i, k: ffn.at[i, pl.ds(128 * k, 128)], "z", own
    )
    next(passed)
    drive(*later)
    feed_back_in(cots, down, grad_hidden)

    def chunk(i):
        feed_chunk(
            i, ffn, gate_up, down, grad_hidden, hidden, turned, ffn_turned, grad_both, grad_ffn, out_part
        )

    right, left = lk.sides("z")
    chunk(own)
    lk.flush()
    next(passed)
    chunk(before)
    one = lk.put(grad_ffn.at[before], from_right, left)
    chunk(after)
    two = lk.put(grad_ffn.at[after], from_left, right)
    next(passed, None)
    chunk(far)
    saved.append(lk.keep(out_part, outs[13]))
    three = lk.put(grad_ffn.at[far, pl.ds(0, 128)], passing.at[0], right)
    four = lk.put(grad_ffn.at[far, pl.ds(128, 128)], passing.at[1], left)
    feed_grads(ffn_turned, grad_both, gate_up, 9)
    saved.append(lk.keep(gate_up, outs[11]))
    three.wait_recv()
    five = lk.put(passing.at[0], from_far.at[0], right)
    four.wait_recv()
    six = lk.put(passing.at[1], from_far.at[1], left)
    feed_grads(turned, cots, down, 4)
    saved.append(lk.keep(down, outs[12]))
    for copy in (one, two, five, six):
        copy.wait_recv()
    for copy in saved:
        copy.wait()
    total = grad_ffn[own].astype(F32) + from_right[...].astype(F32) + from_left[...].astype(F32)
    lin_query[...] = total + flat(from_far[...]).astype(F32)
    lk.keep(lin_query, outs[14]).wait()
    lk.flush()


def forward(*args):
    return pl.pallas_call(
        fwd_kernel,
        out_shape=FWD_OUT,
        in_specs=[ANY] * 7,
        out_specs=[ANY] * len(FWD_OUT),
        scratch_shapes=sems(96) + FWD_SCRATCH,
        compiler_params=pltpu.CompilerParams(
            collective_id=0, has_side_effects=True, vmem_limit_bytes=60 * 2**20
        ),
    )(*args)


BWD_IN = 18
PIECES = (1152, 1152, 512, 512, 512, 512, 512, 640)
BWD_OUT = (
    shape(256, 1024),
    shape(256, 1024, dtype=F32),
    shape(4, 32, WA),
    shape(4, 32, GU),
    shape(DN, 1024),
    shape(32, WA),
    shape(32, GU),
)
BWD_SCRATCH = [
    pltpu.VMEM((4, 4, 2, 32, WA), BF),
    pltpu.VMEM((256, 1024), BF),
    pltpu.VMEM((256, 1024), F32),
    pltpu.VMEM((256, 512), F32),
    pltpu.VMEM((2, 8, 512, 128), BF),
    pltpu.VMEM((2, 8, 512, 128), BF),
    pltpu.VMEM((2, 8, 256, 128), BF),
    pltpu.VMEM((16, 512, 256), BF),
    pltpu.VMEM((256, 1024), BF),
    pltpu.VMEM((256, 1024), F32),
    pltpu.VMEM((8, 1024), F32),
    pltpu.VMEM((4, 256, 1024), BF),
    pltpu.VMEM((256, 1024), F32),
    pltpu.VMEM((256, 1024), BF),
    pltpu.VMEM((256, 1024), BF),
    pltpu.VMEM((256, 128), F32),
]
BWD_WORK = [
    pltpu.VMEM((256, 1024), BF),
    pltpu.VMEM((2, 8, 256, 128), BF),
    pltpu.VMEM((256, 1024), F32),
    pltpu.VMEM((4, 256, 1024), BF),
    pltpu.VMEM((256, 2048), BF),
    pltpu.VMEM((1024, 256), BF),
    pltpu.VMEM((256, 1024), F32),
    pltpu.VMEM((8, 1024), F32),
    pltpu.VMEM((4, 4, 2, 32, WA), BF),
    pltpu.VMEM((4, 4, 32, 1152), BF),
    pltpu.VMEM((4, 4, 32, 1152), BF),
    pltpu.VMEM((256, 1024), BF),
]
Z_RING = [
    pltpu.VMEM((128, 1024), BF),
    pltpu.VMEM((128, 1024), BF),
    pltpu.VMEM((256, 1024), BF),
    pltpu.VMEM((256, 1024), BF),
]


def norm_back(v, g, dy):
    r = row_scale(v)
    gdy = g * dy
    back = r * gdy - v * (r * r * r * jnp.mean(v * gdy, axis=-1, keepdims=True))
    return back, jnp.sum(v * r * dy, axis=0, keepdims=True)


def heads_back(lin, grad, gain, cosine, sine, ones):
    parts = []
    for h in range(2):
        part = grad[:, 128 * h : 128 * h + 128]
        parts.append(part * cosine + halves_swapped(part * sine))
    dy = jnp.concatenate(parts, axis=1)
    r = lax.rsqrt(head_mean(lin * lin, ones) + EPS)
    gdy = dy * gain
    back = r * gdy - lin * (r * r * r * head_mean(lin * gdy, ones))
    return back, jnp.sum(lin * r * dy, axis=0, keepdims=True)


def turned_grads(turned, right, out, start, tiles, base=0):
    def step(j, _):
        got = dot(turned[...], right[:, pl.ds(pl.multiple_of(base + 256 * j, 256), 256)], kind=BF)
        out[:, :, :, :, pl.ds(pl.multiple_of(start + 256 * j, 128), 256)] = got.reshape(4, 4, 2, 32, 256)
        return 0

    lax.fori_loop(0, tiles, step, 0)


def attend_back(queries, keys, values, probs, grad_mixed, grad_queries, grad_kv, tick):
    lane = lanes_of((128, 128))
    lane_keys = lanes_of((512, 128))

    def step(n, _):
        m, j = n // 4, n % 4
        folded = []
        for e in range(2):
            k = 2 * j + e
            i = m * 8 + k
            chance = probs[i]
            back = dot(values[m, k], grad_mixed[m, k], ROWS)
            p = chance.astype(F32)
            p_back = p * back
            grad_scores = (p_back - p * jnp.sum(p_back, axis=0, keepdims=True)).astype(BF)
            got = dot(keys[m, k], grad_scores, TOKENS).T
            cut = pl.ds(pl.multiple_of(128 * k, 128), 128)
            grad_queries[pl.ds(pl.multiple_of(m * 128, 128), 128), cut] = jnp.where(
                lane < 64, got[0:128], got[128:256]
            )
            for v in (dot(grad_scores, queries[m, k]), dot(chance, grad_mixed[m, k])):
                folded.append(v + pltpu.roll(v, 64, 1))
        for s in range(2):
            tile = jnp.where(lane_keys < 64, folded[s], folded[2 + s]).astype(BF)
            cut = pl.ds(pl.multiple_of(512 * s + 128 * j, 128), 128)
            for q in range(4):
                grad_kv[q, pl.ds(pl.multiple_of(m * 128, 128), 128), cut] = tile[128 * q : 128 * q + 128]

        return 0

    lax.fori_loop(0, 4, step, 0)
    tick()
    lax.fori_loop(4, 8, step, 0)


def bwd_kernel(*refs):
    ins, refs = refs[:BWD_IN], refs[BWD_IN:]
    outs, refs = refs[: len(BWD_OUT)], refs[len(BWD_OUT) :]
    lk = Links(*refs[:3])
    refs = refs[3:]
    n = len(BWD_SCRATCH)
    held, refs = refs[:n], refs[n:]
    (
        whole, normed, lin_query, lin_key, keys, values, queries, probs, mixed, middle, gain, out_part, grad_middle,
        upstream, source, table,
    ) = held
    grad_gu, grad_down = ins[16:]
    n = len(BWD_WORK)
    work, refs = refs[:n], refs[n:]
    (
        grad_branch, grad_mixed, grad_queries, grad_kv, grad_lin, turned, grad_normed, gains_back, grad_whole, acc_a,
        acc_b, made,
    ) = work
    z_out, z_kv, refs = refs[:4], refs[4:8], refs[8:]
    down_refs, refs = refs[:10], refs[10:]
    rings = [refs[9 * i : 9 * i + 9] for i in range(len(PIECES))]
    outputs, grad_inputs, a_all, gu_all, down_own, a_own, gu_own = outs
    own, c = lk.z, lk.c

    order = [12, 9, 13, 10, 0, 8, 5, 7, 6, 4, 11, 2, 15, 1, 3, 14]
    loads = {}
    for k in order[:6]:
        loads[k] = lk.keep(ins[k], held[k])
    lk.barrier("xyzc")

    def piece(k, spot, src, out, first, kept=None):
        ring = rings[k]
        return plane_reduce(lk, spot, src, ring[0], (ring[1:5], ring[5:9]), out, first, kept)

    def feed_piece(k, acc, lo, first):
        cols = pl.ds(lo, 1152)
        kept = lk.keep(grad_gu.at[:, :, c, :, cols], acc)
        return piece(
            k, lambda i, j: acc.at[i, j], grad_gu.at[:, :, lk.other, :, cols], gu_own.at[:, cols], first, kept
        )

    def whole_piece(k, lo, first):
        cols = pl.ds(lo, PIECES[k])
        return piece(
            k, lambda i, j: grad_whole.at[i, j, c, :, cols], grad_whole.at[:, :, lk.other, :, cols],
            a_own.at[:, cols], first,
        )

    def feed_chain():
        parts = [feed_piece(0, acc_a, 0, "y"), feed_piece(1, acc_b, 1152, "x")]
        while parts:
            parts = [s for s in parts if next(s, "end") != "end"]
            yield 1
        yield from line_gather(lk, gu_own, gu_all, 16)

    def out_chain():
        yield from ring_reduce(
            lk, lambda i: out_part.at[i], lambda i, k: out_part.at[i, pl.ds(128 * k, 128)], z_out, "z", own
        )
        made[...] = (middle[...] + out_part[own].astype(F32)).astype(BF)
        done = lk.keep(made, outputs)
        yield 1
        done.wait()

    behind = [feed_chain(), down_reduce(lk, grad_down, down_refs, down_own)]

    def tick():
        for s in list(behind):
            if next(s, "end") == "end":
                behind.remove(s)

    tick()
    for k in order[6:]:
        loads[k] = lk.keep(ins[k], held[k])

    def need(*names):
        for k in names:
            loads.pop(k).wait()

    need(12, 9, 13, 10)
    back, row = norm_back(middle[...], gain[1:2], grad_middle[...])
    total = upstream[...].astype(F32) + back
    grad_middle[...] = total
    grad_branch[...] = total.astype(BF)
    gains_back[1:2] = row
    need(0, 8)
    tick()
    turned[...] = mixed[...].T
    turned_grads(turned, grad_branch, grad_whole, 2176, 4)
    behind += [whole_piece(2, 2176, "y"), whole_piece(3, 2688, "x")]
    tick()
    lane = lanes_of((256, 128))

    def back_mixed(j, _):
        got = dot(grad_branch[...], flat(whole[j, :, :, :, pl.ds(2176, 1024)]), ROWS)
        for h in range(2):
            r = got[:, 128 * h : 128 * h + 128]
            first = jnp.where(lane < 64, r, 0.0).astype(BF)
            second = jnp.where(lane < 64, 0.0, r).astype(BF)
            for m in range(2):
                grad_mixed[m, 2 * j + h, 0:128] = first[128 * m : 128 * m + 128]
                grad_mixed[m, 2 * j + h, 128:256] = second[128 * m : 128 * m + 128]
        return 0

    lax.fori_loop(0, 4, back_mixed, 0)
    need(5, 7, 6, 4, 11)
    behind.append(out_chain())
    tick()
    attend_back(queries, keys, values, probs, grad_mixed, grad_queries, grad_kv, tick)
    kv_sum = ring_reduce(
        lk, lambda i: grad_kv.at[i], lambda i, k: grad_kv.at[i, pl.ds(128 * k, 128)], z_kv, "z", own
    )
    next(kv_sum)
    tick()
    need(2, 15, 1)
    ones = head_ones()
    cosine, sine = angle_tables(table[...])

    def back_query(j, _):
        cut = pl.ds(pl.multiple_of(256 * j, 256), 256)
        grad = grad_queries[:, cut] * HEAD_SIZE ** (-0.5)
        got, line = heads_back(lin_query[:, cut], grad, gain[2:3, 0:256], cosine, sine, ones)
        grad_lin[:, cut] = got.astype(BF)
        gains_back[2:3, cut] = line
        return 0

    lax.fori_loop(0, 4, back_query, 0)
    turned[...] = normed[...].T
    turned_grads(turned, grad_lin, grad_whole, 0, 4)
    behind += [whole_piece(4, 0, "y"), whole_piece(5, 512, "x")]
    tick()
    next(kv_sum)

    def back_normed(j, _):
        grad_normed[:, pl.ds(pl.multiple_of(256 * j, 256), 256)] = dot(
            grad_lin[:, 0:1024], flat(whole[j, :, :, :, pl.ds(0, 1024)]), ROWS
        )
        return 0

    lax.fori_loop(0, 4, back_normed, 0)
    need(3, 14)
    tick()
    next(kv_sum, None)

    def back_key(j, _):
        cut = pl.ds(pl.multiple_of(256 * j, 256), 256)
        grad = grad_kv[own, :, cut].astype(F32)
        got, line = heads_back(lin_key[:, cut], grad, gain[3:4, 0:256], cosine, sine, ones)
        grad_lin[:, pl.ds(pl.multiple_of(1024 + 256 * j, 256), 256)] = got.astype(BF)
        gains_back[3:4, cut] = line
        return 0

    lax.fori_loop(0, 2, back_key, 0)
    grad_lin[:, 1536:2048] = grad_kv[own, :, 512:1024]
    turned_grads(turned, grad_lin, grad_whole, 1024, 4, 1024)

    def more_normed(j, _):
        cut = pl.ds(pl.multiple_of(256 * j, 256), 256)
        grad_normed[:, cut] = grad_normed[:, cut] + dot(
            grad_lin[:, 1024:2048], flat(whole[j, :, :, :, pl.ds(1024, 1024)]), ROWS
        )
        return 0

    lax.fori_loop(0, 4, more_normed, 0)
    back, row = norm_back(source[...].astype(F32), gain[0:1], grad_normed[...])
    gains_back[0:1] = row
    grad_normed[...] = grad_middle[...] + back

    small = [jnp.zeros((1, 128), F32)] * 2
    for s, tiles in ((0, 8), (1, 4)):
        for k in range(tiles):
            small[s] = small[s] + gains_back[2 + s : 3 + s, 128 * k : 128 * k + 128]
        small[s] = small[s] + pltpu.roll(jnp.broadcast_to(small[s], (8, 128)), 64, 1)[0:1]
    heads = jnp.where(lanes_of((1, 128)) < 64, small[0], small[1])
    line = lax.broadcasted_iota(jnp.int32, (32, 128), 0)
    for k in range(8):
        cut = slice(128 * k, 128 * k + 128)
        block = jnp.where(line == 8, gains_back[0:1, cut], 0.0)
        block = jnp.where(line == 16, gains_back[1:2, cut], block)
        block = jnp.where(line == 0, heads, block).astype(BF)
        for d in range(4 * k, 4 * k + 4):
            grad_whole[d // 8, (d // 2) % 4, d % 2, :, 2048:2176] = block
    behind += [whole_piece(6, 1024, "y"), whole_piece(7, 1536, "x")]
    drive(*behind)
    final = lk.keep(grad_normed, grad_inputs)
    drive(line_gather(lk, a_own, a_all, 16))
    final.wait()
    lk.flush()


def backward(*args):
    return pl.pallas_call(
        bwd_kernel,
        out_shape=BWD_OUT,
        in_specs=[ANY] * BWD_IN,
        out_specs=[ANY] * len(BWD_OUT),
        scratch_shapes=sems(128) + BWD_SCRATCH + BWD_WORK + Z_RING * 2 + down_scratch()
        + [v for cols in PIECES for v in ring_scratch(cols)],
        compiler_params=pltpu.CompilerParams(
            collective_id=1, has_side_effects=True, vmem_limit_bytes=62 * 2**20
        ),
    )(*args)


def body(
    inputs, starts, w_query, key_weight, value_weight, w_out, w_gate, w_up, w_down,
    prenorm, midnorm, querynorm, keynorm, cotangent,
):
    z = lax.axis_index("seq")
    dp = lax.axis_index("dp")
    lane = jnp.arange(128)[None, :]
    line = jnp.arange(32)[:, None]

    def spread(v, row, start):
        here = jnp.pad(v, (0, 128 - v.shape[0]))
        return jnp.where(line == row, jnp.roll(here, start)[None, :], 0)

    both = dp % 4 * 32
    gains = spread(prenorm, 8 + dp // 4, both) + spread(midnorm, 16 + dp // 4, both)
    for row, v in ((0, querynorm), (1, keynorm)):
        gains = gains + spread(v, row, 2 * dp) + spread(v, row, 2 * dp + 64)
    wa = jnp.concatenate([w_query, key_weight, value_weight, gains, w_out], axis=1)
    gu = jnp.concatenate(
        [lax.dynamic_slice(w, (0, z * 1152), (32, 1152)) for w in (w_gate, w_up)], axis=1
    )
    pos = z * 128 + jnp.arange(128, dtype=jnp.int32)
    inside = pos - starts[:, 0]
    frequency = ROPE_BASE ** (-(jnp.arange(32, dtype=F32) * 2.0 / 64))
    angle = inside.reshape(256, 1).astype(F32) * frequency[None, :]
    cosine, sine = jnp.cos(angle), jnp.sin(angle)
    tab = jnp.concatenate([cosine, cosine, -sine, sine], axis=1)
    source = inputs.reshape(256, 1024)
    upstream = cotangent.reshape(256, 1024)
    (
        whole, normed, lin_query, lin_key, keys, values, queries, probs, mixed, middle, gain, grad_gu, grad_down,
        out_part, grad_ffn,
    ) = forward(wa, gu, w_down, source, upstream, tab, starts[:, 0])
    outputs, grad_inputs, own_whole, own_gu, own_down, _, _ = backward(
        whole, normed, lin_query, lin_key, keys, values, queries, probs, mixed, middle, gain, out_part, grad_ffn,
        upstream, source, tab, grad_gu, grad_down,
    )
    own = jnp.sum(own_whole.astype(F32), axis=0)
    own_gu = own_gu.astype(F32).transpose(1, 0, 2)
    grad_gains = own[:, 2048:2176]
    return (
        outputs.reshape(2, 1, 128, 1024),
        grad_inputs.reshape(2, 1, 128, 1024),
        own[:, :1024],
        own[:, 1024:1536],
        own[:, 1536:2048],
        own[:, 2176:],
        own_gu[:, :, :1152].reshape(32, 4608),
        own_gu[:, :, 1152:].reshape(32, 4608),
        own_down.astype(F32),
        lax.dynamic_slice(grad_gains, (8, both), (1, 32))[0],
        lax.dynamic_slice(grad_gains, (16, both), (1, 32))[0],
        lax.dynamic_slice(grad_gains, (0, 2 * dp), (1, 2))[0],
        lax.dynamic_slice(grad_gains, (0, 64 + 2 * dp), (1, 2))[0],
    )


def solution(mesh):
    tokens, matrix, vector = P(None, "dp", "seq", None), P("dp", None), P("dp")
    return jax.shard_map(
        body,
        mesh=mesh,
        in_specs=(tokens, P(None, "dp", "seq")) + (matrix,) * 7 + (vector,) * 4 + (tokens,),
        out_specs=(tokens, tokens) + (matrix,) * 7 + (vector,) * 4,
        check_vma=False,
    )
```

profile of v0, /device:TPU:0, one launch (start us, length us, event | category | flops | bytes accessed | tf_op | source)
XLA Modules:
  0.0 265.8 jit_solution(11346789848360861756)
XLA Ops:
  0.7 0.7 pad.16
  1.4 0.1 dynamic_slice.32
  1.5 0.7 pad.17
  2.2 0.1 dynamic_slice.33
  2.3 0.7 pad.18
  2.9 0.7 pad.19
  3.6 0.1 fusion.6
  3.7 0.7 fusion.1
  4.4 0.9 constant_dynamic-slice_fusion.2
  5.3 0.7 pad_maximum_fusion.gu
  6.0 0.8 constant_dynamic-update-slice_fusion.4
  6.8 0.8 constant_dynamic-update-slice_fusion.3
  7.6 0.8 constant_dynamic-update-slice_fusion.2
  8.4 0.1 constant_dynamic-update-slice_fusion.1
  8.5 0.8 constant_dynamic-update-slice_fusion.wa
  9.3 0.0 copy-start.3
  9.3 0.5 multiply_cosine_fusion
  9.8 0.8 pad_maximum_fusion.1.tab.refs_15_
  10.7 0.0 copy-done.3
  10.7 128.9 %shard_map.237 = (bf16[4,4,2,32,3200]{4,3,2,1,0:T(8,128)(2,1)}, bf16[256,1024]{1,0:T(8,128)(2,1)}, f32[256,1024]{1,0:T(8,128)}, f32[256,512]{1,0:T(8,128)}, bf16...) custom-call(bf16[32,3200]{1,0:T(8,128)(2,1)} %copy-done.3, ...), custom_call_target="tpu_custom_call" | custom-call | tf_op jit(solution)/shard_map/pallas_call | solution.py:761
  139.6 117.7 %shard_map.238 = (bf16[256,1024]{1,0:T(8,128)(2,1)}, f32[256,1024]{1,0:T(8,128)}, bf16[4,32,3200]{2,1,0:T(8,128)(2,1)}, bf16[4,32,2304]{2,1,0:T(8,128)(2,1)}, bf...) custom-call(bf16[4,4,2,32,3200]{4,3,2,1,0:T(8,128)(2,1)} %get-tuple-element.34.refs_0_, ...), custom_call_target="tpu_custom_call" | custom-call | tf_op jit(solution)/shard_map/pallas_call | solution.py:1078
  257.3 0.0 copy-start.4
  257.3 0.0 copy-start.1
  257.3 1.4 convert_reduce_fusion
  258.7 0.6 fusion.3
  259.3 0.6 dynamic-slice_bitcast_fusion
  259.9 0.7 fusion.5
  260.5 0.7 fusion.4
  261.2 0.0 copy-done.4
  261.2 0.9 convert_element_type.32
  262.1 0.0 copy-done.1
  262.1 0.1 convert_bitcast_fusion
  262.2 0.0 copy-start.2
  262.2 0.1 slice_bitcast_fusion
  262.3 0.0 copy-start
  262.3 0.9 copy.39
  263.2 0.9 copy.38
  264.0 0.0 copy-done.2
  264.1 0.8 copy.46
  264.8 0.0 copy-done
  264.8 1.0 copy.47
  (9 shorter events, 0.1 us)
Async XLA Ops:
  9.3 1.4 copy-start.3
  257.3 4.0 %copy-start.4 = (bf16[144,1024]{1,0:T(8,128)(2,1)S(1)}, bf16[144,1024]{1,0:T(8,128)(2,1)}, u32[]{:S(2)}) copy-start(bf16[144,1024]{1,0:T(8,128)(2,1)} %get-tuple-element.53) | copy-start | bytes 884740
  257.3 4.8 %copy-start.1 = (bf16[4,32,2304]{2,1,0:T(8,128)(2,1)S(1)}, bf16[4,32,2304]{2,1,0:T(8,128)(2,1)}, u32[]{:S(2)}) copy-start(bf16[4,32,2304]{2,1,0:T(8,128)(2,1)} %get-tuple-element.52) | copy-start | bytes 1769476
  262.2 1.8 copy-start.2
  262.3 2.5 copy-start
where the time goes:
time: 267 us; the launch traced here: 266 us
  Pallas kernels  247 us (93%)
  local copies, waits for them, and re-layouts  13.2 us (5%)
  other arithmetic  5.21 us (2%)
    pallas_call x1, Pallas kernels, forward(): pl.pallas_call(fwd_kernel, out_shape=FWD_OUT, in_specs=[ANY] * 7, out_spe...  129 us
    pallas_call x1, Pallas kernels, backward(): pl.pallas_call(bwd_kernel, out_shape=BWD_OUT, in_specs=[ANY] * BWD_IN, ou...  118 us

commit v1 on v0

--- a/solution.py
+++ b/solution.py
@@ -68,6 +68,7 @@
             device_id_type=MESH,
         )
         self.n += 1
+        assert self.n <= self.send.shape[0]
         return copy
 
     def put(self, src, dst, to):
@@ -79,6 +80,7 @@
     def keep(self, src, dst):
         copy = pltpu.make_async_copy(src, dst, self.local.at[self.m])
         self.m += 1
+        assert self.m <= self.local.shape[0]
         copy.start()
         return copy
 
@@ -299,9 +301,8 @@
     else:
         yield from ring_reduce(lk, lambda i: spot(i, every), lambda i, k: spot(i, pair(k)), one, "x", x)
         yield from ring_reduce(lk, lambda j: spot(x, j), lambda j, k: rows(spot(x, j), k), two, "y", y)
-    done = lk.keep(spot(x, y), out)
     yield 1
-    done.wait()
+    yield from line_gather(lk, spot(x, y), out, 16)
 
 
 def ring_scratch(cols):
@@ -532,38 +533,56 @@
     lax.fori_loop(0, 4, step, 0)
 
 
-def attend(queries, keys, values, starts, probs, mixed, own):
+def attend(m, queries, keys, values, starts, probs, mixed, own):
     key_pos = lax.broadcasted_iota(jnp.int32, (512, 256), 0)
     query_pos = own * 128 + lax.broadcasted_iota(jnp.int32, (1, 256), 1) % 128
     lane = lanes_of((128, 128))
 
-    def step(i, _):
-        m, k = i // 8, i % 8
-        row = starts[pl.ds(m, 1)]
-        begin = jnp.concatenate([row, row], axis=1)
+    row = starts[m : m + 1]
+    begin = jnp.concatenate([row, row], axis=1)
+
+    def step(k, _):
         scores = dot(keys[m, k], queries[m, k], ROWS)
         scores = jnp.where((key_pos <= query_pos) & (key_pos >= begin), scores, -1e30)
         raised = jnp.exp(scores - jnp.max(scores, axis=0, keepdims=True))
         chance = (raised * (1.0 / jnp.sum(raised, axis=0, keepdims=True))).astype(BF)
-        probs[i] = chance
+        probs[8 * m + k] = chance
         got = dot(values[m, k], chance, TOKENS).T
         both = jnp.where(lane < 64, got[0:128], got[128:256]).astype(BF)
-        mixed[pl.ds(pl.multiple_of(m * 128, 128), 128), pl.ds(pl.multiple_of(k * 128, 128), 128)] = both
-        return 0
-
-    lax.fori_loop(0, 16, step, 0)
-
-
-def out_project(whole, source, gain, mixed, middle, normed_ffn, own):
+        mixed[128 * m : 128 * m + 128, pl.ds(pl.multiple_of(k * 128, 128), 128)] = both
+        return 0
+
+    lax.fori_loop(0, 8, step, 0)
+
+
+def out_project(m, whole, sources, gain, mixed, middle, normed_ffn, own):
+    rows = pl.ds(128 * m, 128)
+
     def step(j, _):
         cut = pl.ds(pl.multiple_of(256 * j, 256), 256)
         w = flat(whole[:, :, :, :, pl.ds(pl.multiple_of(2176 + 256 * j, 128), 256)])
-        middle[:, cut] = source[:, cut].astype(F32) + dot(mixed[...], w)
+        middle[rows, cut] = sources[own, rows, cut].astype(F32) + dot(mixed[rows], w)
         return 0
 
     lax.fori_loop(0, 4, step, 0)
-    mid = middle[...]
-    normed_ffn[own] = (mid * row_scale(mid) * gain[1:2]).astype(BF)
+    mid = middle[rows]
+    normed_ffn[own, rows] = (mid * row_scale(mid) * gain[1:2]).astype(BF)
+
+
+def own_gains(params, dp):
+    row = jnp.broadcast_to(params, (32, 128))
+    line = lax.broadcasted_iota(jnp.int32, (32, 128), 0)
+    lane = lanes_of((32, 128))
+    spot = dp % 4 * 32
+    window = (lane >= spot) & (lane < spot + 32)
+    got = jnp.where((line == 8 + dp // 4) & window, pltpu.roll(row, spot, 1), 0.0)
+    got = got + jnp.where((line == 16 + dp // 4) & window, pltpu.roll(row, (spot + 96) % 128, 1), 0.0)
+    pair = (lane % 64 >= 2 * dp) & (lane % 64 < 2 * dp + 2)
+    for k in range(2):
+        low = pltpu.roll(row, (2 * dp + 64 - 2 * k) % 128, 1)
+        high = pltpu.roll(row, (2 * dp + 128 - 2 * k) % 128, 1)
+        got = got + jnp.where((line == k) & pair, jnp.where(lane < 64, low, high), 0.0)
+    return got.astype(BF)
 
 
 def feed_back_in(cots, down, grad_hidden):
@@ -642,9 +661,12 @@
     pltpu.VMEM((4, 256, 1024), BF),
     pltpu.VMEM((256, 1024), BF),
     pltpu.VMEM((256, 1024), BF),
-    pltpu.VMEM((2, 128, 1024), BF),
-    pltpu.VMEM((2, 128, 1024), BF),
+    pltpu.VMEM((4, 64, 1024), BF),
+    pltpu.VMEM((4, 64, 1024), BF),
     pltpu.VMEM((2, 128), jnp.int32),
+    pltpu.VMEM((32, WA), BF),
+    pltpu.VMEM((32, GU), BF),
+    pltpu.VMEM((1, 128), F32),
 ]
 
 FWD_OUT = (
@@ -666,60 +688,95 @@
 )
 
 
-def fwd_kernel(wa, gu, dn, x, cot, tab, starts_hbm, *refs):
+FWD_IN = 12
+
+
+def go(*steps):
+    for s in steps:
+        next(s, None)
+
+
+def fwd_kernel(*refs):
+    w_query, key_weight, value_weight, w_out, w_gate, w_up, dn, x, cot, tab, starts_hbm, params_hbm = refs[:FWD_IN]
+    refs = refs[FWD_IN:]
     outs, refs = refs[: len(FWD_OUT)], refs[len(FWD_OUT) :]
     lk = Links(*refs[:3])
     (
         whole, gate_up, down, sources, tables, cots, ffn, normed, lin_query, lin_key, keys, values, queries,
         probs, mixed, middle, gain, grad_hidden, hidden, turned, ffn_turned, grad_both, grad_ffn, out_part,
-        from_right, from_left, passing, from_far, starts,
+        from_right, from_left, passing, from_far, starts, wa, gu, own_params,
     ) = refs[3:]
     own = lk.z
-    before, after, far = (own + 3) % 4, (own + 1) % 4, (own + 2) % 4
+    before, after, far = lk.ring["z"]
+    quarter = pl.ds(pl.multiple_of(own * 1152, 128), 1152)
+    staged = [
+        lk.keep(params_hbm, own_params),
+        lk.keep(starts_hbm, starts),
+        lk.keep(w_query, wa.at[:, pl.ds(0, 1024)]),
+        lk.keep(key_weight, wa.at[:, pl.ds(1024, 512)]),
+        lk.keep(value_weight, wa.at[:, pl.ds(1536, 512)]),
+        lk.keep(w_out, wa.at[:, pl.ds(2176, 1024)]),
+        lk.keep(w_gate.at[:, quarter], gu.at[:, pl.ds(0, 1152)]),
+        lk.keep(w_up.at[:, quarter], gu.at[:, pl.ds(1152, 1152)]),
+    ]
+    staged[0].wait()
+    wa[:, 2048:2176] = own_gains(own_params[...], lax.axis_index("dp"))
+    for copy in staged[1:]:
+        copy.wait()
     lk.barrier("xyzc")
-    first = [
-        plane_gather(lk, wa, whole, "x", 0, 1536),
-        plane_gather(lk, wa, whole, "y", 1536, WA),
-        line_gather(lk, tab, tables, 128),
-        line_gather(lk, x, sources, 128),
-    ]
-    later = [
-        plane_gather(lk, gu, gate_up, "x", 0, 1152),
-        plane_gather(lk, gu, gate_up, "y", 1152, GU),
-        down_gather(lk, dn, down),
-        line_gather(lk, cot, cots, 128),
-    ]
-    for s in first + later[:3]:
-        next(s)
-    saved = [lk.keep(starts_hbm, starts)]
-    saved[0].wait()
-    saved = []
-    drive(*first)
-
-    def tick():
-        for s in later:
-            next(s, None)
-
-    tick()
+    a1 = plane_gather(lk, wa, whole, "x", 0, 1536)
+    a2 = plane_gather(lk, wa, whole, "y", 1536, WA)
+    t1 = line_gather(lk, tab, tables, 128)
+    x1 = line_gather(lk, x, sources, 128)
+    g1 = plane_gather(lk, gu, gate_up, "x", 0, 1152)
+    g2 = plane_gather(lk, gu, gate_up, "y", 1152, GU)
+    d1 = down_gather(lk, dn, down)
+    c1 = line_gather(lk, cot, cots, 128)
+    go(a1, a2, t1, x1)
+    go(a1, a2)
+    go(g1, g2)
+    go(a1, a2)
+    go(t1, x1)
+    go(a1, a2)
+    go(g1, g2)
+    go(a1, a2)
+    go(g1, g2)
+    go(d1)
+    go(t1, x1)
+    go(c1)
+    drive(a1, a2, t1, x1)
     gain_rows(whole, gain)
-    saved.append(lk.keep(whole, outs[0]))
+    saved = [lk.keep(whole, outs[0])]
     keys_values(whole, sources, tables, gain, normed, keys, values, lin_key, own)
-    tick()
+    go(g1, g2)
+    go(d1)
+    go(c1)
     own_queries(whole, tables, gain, normed, lin_query, queries, own)
     for k, ref in enumerate((normed.at[own], lin_query, lin_key, keys, values, queries)):
         saved.append(lk.keep(ref, outs[1 + k]))
-    tick()
-    attend(queries, keys, values, starts, probs, mixed, own)
-    tick()
-    out_project(whole, sources.at[own], gain, mixed, middle, ffn, own)
+    passed = []
+    for m in range(2):
+        attend(m, queries, keys, values, starts, probs, mixed, own)
+        out_project(m, whole, sources, gain, mixed, middle, ffn, own)
+        rows = pl.ds(128 * m, 128)
+
+        def part(i, k, m=m):
+            return ffn.at[i, pl.ds(128 * m + 64 * k, 64)]
+
+        passed.append(
+            ring_gather(lk, ffn.at[own, rows], lambda i, rows=rows: ffn.at[i, rows], part, "z", own)
+        )
+        go(passed[m])
+        if m == 0:
+            go(g1, g2)
+            go(d1)
+            go(c1)
+    go(passed[0])
     for k, ref in enumerate((probs, mixed, middle, gain)):
         saved.append(lk.keep(ref, outs[7 + k]))
-    passed = ring_gather(
-        lk, ffn.at[own], lambda i: ffn.at[i], lambda i, k: ffn.at[i, pl.ds(128 * k, 128)], "z", own
-    )
-    next(passed)
-    drive(*later)
+    drive(g1, g2, d1, c1)
     feed_back_in(cots, down, grad_hidden)
+    go(*passed)
 
     def chunk(i):
         feed_chunk(
@@ -729,25 +786,25 @@
     right, left = lk.sides("z")
     chunk(own)
     lk.flush()
-    next(passed)
     chunk(before)
-    one = lk.put(grad_ffn.at[before], from_right, left)
+    sent = [lk.put(grad_ffn.at[before], from_right, left)]
     chunk(after)
-    two = lk.put(grad_ffn.at[after], from_left, right)
-    next(passed, None)
+    sent.append(lk.put(grad_ffn.at[after], from_left, right))
+    go(*passed)
     chunk(far)
     saved.append(lk.keep(out_part, outs[13]))
-    three = lk.put(grad_ffn.at[far, pl.ds(0, 128)], passing.at[0], right)
-    four = lk.put(grad_ffn.at[far, pl.ds(128, 128)], passing.at[1], left)
+    hops = []
+    for k in range(4):
+        to = right if k % 2 == 0 else left
+        hops.append((lk.put(grad_ffn.at[far, pl.ds(64 * k, 64)], passing.at[k], to), to))
     feed_grads(ffn_turned, grad_both, gate_up, 9)
     saved.append(lk.keep(gate_up, outs[11]))
-    three.wait_recv()
-    five = lk.put(passing.at[0], from_far.at[0], right)
-    four.wait_recv()
-    six = lk.put(passing.at[1], from_far.at[1], left)
+    for k, (copy, to) in enumerate(hops):
+        copy.wait_recv()
+        sent.append(lk.put(passing.at[k], from_far.at[k], to))
     feed_grads(turned, cots, down, 4)
     saved.append(lk.keep(down, outs[12]))
-    for copy in (one, two, five, six):
+    for copy in sent:
         copy.wait_recv()
     for copy in saved:
         copy.wait()
@@ -761,7 +818,7 @@
     return pl.pallas_call(
         fwd_kernel,
         out_shape=FWD_OUT,
-        in_specs=[ANY] * 7,
+        in_specs=[ANY] * FWD_IN,
         out_specs=[ANY] * len(FWD_OUT),
         scratch_shapes=sems(96) + FWD_SCRATCH,
         compiler_params=pltpu.CompilerParams(
@@ -778,8 +835,6 @@
     shape(4, 32, WA),
     shape(4, 32, GU),
     shape(DN, 1024),
-    shape(32, WA),
-    shape(32, GU),
 )
 BWD_SCRATCH = [
     pltpu.VMEM((4, 4, 2, 32, WA), BF),
@@ -819,6 +874,12 @@
     pltpu.VMEM((256, 1024), BF),
     pltpu.VMEM((256, 1024), BF),
 ]
+Z_HALF = [
+    pltpu.VMEM((64, 1024), BF),
+    pltpu.VMEM((64, 1024), BF),
+    pltpu.VMEM((128, 1024), BF),
+    pltpu.VMEM((128, 1024), BF),
+]
 
 
 def norm_back(v, g, dy):
@@ -849,12 +910,11 @@
     lax.fori_loop(0, tiles, step, 0)
 
 
-def attend_back(queries, keys, values, probs, grad_mixed, grad_queries, grad_kv, tick):
+def attend_back(m, queries, keys, values, probs, grad_mixed, grad_queries, grad_kv):
     lane = lanes_of((128, 128))
     lane_keys = lanes_of((512, 128))
 
-    def step(n, _):
-        m, j = n // 4, n % 4
+    def step(j, _):
         folded = []
         for e in range(2):
             k = 2 * j + e
@@ -866,7 +926,7 @@
             grad_scores = (p_back - p * jnp.sum(p_back, axis=0, keepdims=True)).astype(BF)
             got = dot(keys[m, k], grad_scores, TOKENS).T
             cut = pl.ds(pl.multiple_of(128 * k, 128), 128)
-            grad_queries[pl.ds(pl.multiple_of(m * 128, 128), 128), cut] = jnp.where(
+            grad_queries[pl.ds(128 * m, 128), cut] = jnp.where(
                 lane < 64, got[0:128], got[128:256]
             )
             for v in (dot(grad_scores, queries[m, k]), dot(chance, grad_mixed[m, k])):
@@ -875,13 +935,11 @@
             tile = jnp.where(lane_keys < 64, folded[s], folded[2 + s]).astype(BF)
             cut = pl.ds(pl.multiple_of(512 * s + 128 * j, 128), 128)
             for q in range(4):
-                grad_kv[q, pl.ds(pl.multiple_of(m * 128, 128), 128), cut] = tile[128 * q : 128 * q + 128]
+                grad_kv[q, pl.ds(128 * m, 128), cut] = tile[128 * q : 128 * q + 128]
 
         return 0
 
     lax.fori_loop(0, 4, step, 0)
-    tick()
-    lax.fori_loop(4, 8, step, 0)
 
 
 def bwd_kernel(*refs):
@@ -902,10 +960,10 @@
         grad_branch, grad_mixed, grad_queries, grad_kv, grad_lin, turned, grad_normed, gains_back, grad_whole, acc_a,
         acc_b, made,
     ) = work
-    z_out, z_kv, refs = refs[:4], refs[4:8], refs[8:]
+    z_out, z_kv, refs = refs[:4], refs[4:12], refs[12:]
     down_refs, refs = refs[:10], refs[10:]
     rings = [refs[9 * i : 9 * i + 9] for i in range(len(PIECES))]
-    outputs, grad_inputs, a_all, gu_all, down_own, a_own, gu_own = outs
+    outputs, grad_inputs, a_all, gu_all, down_own = outs
     own, c = lk.z, lk.c
 
     order = [12, 9, 13, 10, 0, 8, 5, 7, 6, 4, 11, 2, 15, 1, 3, 14]
@@ -922,22 +980,15 @@
         cols = pl.ds(lo, 1152)
         kept = lk.keep(grad_gu.at[:, :, c, :, cols], acc)
         return piece(
-            k, lambda i, j: acc.at[i, j], grad_gu.at[:, :, lk.other, :, cols], gu_own.at[:, cols], first, kept
+            k, lambda i, j: acc.at[i, j], grad_gu.at[:, :, lk.other, :, cols], gu_all.at[:, :, cols], first, kept
         )
 
     def whole_piece(k, lo, first):
         cols = pl.ds(lo, PIECES[k])
         return piece(
             k, lambda i, j: grad_whole.at[i, j, c, :, cols], grad_whole.at[:, :, lk.other, :, cols],
-            a_own.at[:, cols], first,
+            a_all.at[:, :, cols], first,
         )
-
-    def feed_chain():
-        parts = [feed_piece(0, acc_a, 0, "y"), feed_piece(1, acc_b, 1152, "x")]
-        while parts:
-            parts = [s for s in parts if next(s, "end") != "end"]
-            yield 1
-        yield from line_gather(lk, gu_own, gu_all, 16)
 
     def out_chain():
         yield from ring_reduce(
@@ -948,21 +999,15 @@
         yield 1
         done.wait()
 
-    behind = [feed_chain(), down_reduce(lk, grad_down, down_refs, down_own)]
-
-    def tick():
-        for s in list(behind):
-            if next(s, "end") == "end":
-                behind.remove(s)
-
-    tick()
-    for k in order[6:]:
-        loads[k] = lk.keep(ins[k], held[k])
-
     def need(*names):
         for k in names:
             loads.pop(k).wait()
 
+    f1, f2 = feed_piece(0, acc_a, 0, "y"), feed_piece(1, acc_b, 1152, "x")
+    d1 = down_reduce(lk, grad_down, down_refs, down_own)
+    go(f1, f2, d1)
+    for k in order[6:]:
+        loads[k] = lk.keep(ins[k], held[k])
     need(12, 9, 13, 10)
     back, row = norm_back(middle[...], gain[1:2], grad_middle[...])
     total = upstream[...].astype(F32) + back
@@ -970,11 +1015,6 @@
     grad_branch[...] = total.astype(BF)
     gains_back[1:2] = row
     need(0, 8)
-    tick()
-    turned[...] = mixed[...].T
-    turned_grads(turned, grad_branch, grad_whole, 2176, 4)
-    behind += [whole_piece(2, 2176, "y"), whole_piece(3, 2688, "x")]
-    tick()
     lane = lanes_of((256, 128))
 
     def back_mixed(j, _):
@@ -989,15 +1029,27 @@
         return 0
 
     lax.fori_loop(0, 4, back_mixed, 0)
-    need(5, 7, 6, 4, 11)
-    behind.append(out_chain())
-    tick()
-    attend_back(queries, keys, values, probs, grad_mixed, grad_queries, grad_kv, tick)
-    kv_sum = ring_reduce(
-        lk, lambda i: grad_kv.at[i], lambda i, k: grad_kv.at[i, pl.ds(128 * k, 128)], z_kv, "z", own
-    )
-    next(kv_sum)
-    tick()
+    go(f1, f2, d1)
+    need(5, 7, 6, 4)
+    z_kv_m = []
+    for m in range(2):
+        attend_back(m, queries, keys, values, probs, grad_mixed, grad_queries, grad_kv)
+        rows = pl.ds(128 * m, 128)
+
+        def part(i, k, m=m):
+            return grad_kv.at[i, pl.ds(128 * m + 64 * k, 64)]
+
+        z_kv_m.append(
+            ring_reduce(lk, lambda i, rows=rows: grad_kv.at[i, rows], part, z_kv[4 * m : 4 * m + 4], "z", own)
+        )
+        go(z_kv_m[m])
+        go(f1, f2, d1)
+    turned[...] = mixed[...].T
+    turned_grads(turned, grad_branch, grad_whole, 2176, 4)
+    p2, p3 = whole_piece(2, 2176, "y"), whole_piece(3, 2688, "x")
+    go(p2, p3)
+    go(*z_kv_m)
+    go(f1, f2, d1)
     need(2, 15, 1)
     ones = head_ones()
     cosine, sine = angle_tables(table[...])
@@ -1011,22 +1063,16 @@
         return 0
 
     lax.fori_loop(0, 4, back_query, 0)
+    go(p2, p3)
+    go(f1, f2, d1)
     turned[...] = normed[...].T
     turned_grads(turned, grad_lin, grad_whole, 0, 4)
-    behind += [whole_piece(4, 0, "y"), whole_piece(5, 512, "x")]
-    tick()
-    next(kv_sum)
-
-    def back_normed(j, _):
-        grad_normed[:, pl.ds(pl.multiple_of(256 * j, 256), 256)] = dot(
-            grad_lin[:, 0:1024], flat(whole[j, :, :, :, pl.ds(0, 1024)]), ROWS
-        )
-        return 0
-
-    lax.fori_loop(0, 4, back_normed, 0)
-    need(3, 14)
-    tick()
-    next(kv_sum, None)
+    p4, p5 = whole_piece(4, 0, "y"), whole_piece(5, 512, "x")
+    go(p4, p5)
+    go(p2, p3)
+    go(f1, f2, d1)
+    need(3, 14, 11)
+    drive(*z_kv_m)
 
     def back_key(j, _):
         cut = pl.ds(pl.multiple_of(256 * j, 256), 256)
@@ -1038,20 +1084,17 @@
 
     lax.fori_loop(0, 2, back_key, 0)
     grad_lin[:, 1536:2048] = grad_kv[own, :, 512:1024]
-    turned_grads(turned, grad_lin, grad_whole, 1024, 4, 1024)
-
-    def more_normed(j, _):
-        cut = pl.ds(pl.multiple_of(256 * j, 256), 256)
-        grad_normed[:, cut] = grad_normed[:, cut] + dot(
-            grad_lin[:, 1024:2048], flat(whole[j, :, :, :, pl.ds(1024, 1024)]), ROWS
+
+    def back_normed(j, _):
+        grad_normed[:, pl.ds(pl.multiple_of(256 * j, 256), 256)] = dot(
+            grad_lin[...], flat(whole[j, :, :, :, pl.ds(0, 2048)]), ROWS
         )
         return 0
 
-    lax.fori_loop(0, 4, more_normed, 0)
+    lax.fori_loop(0, 4, back_normed, 0)
     back, row = norm_back(source[...].astype(F32), gain[0:1], grad_normed[...])
     gains_back[0:1] = row
     grad_normed[...] = grad_middle[...] + back
-
     small = [jnp.zeros((1, 128), F32)] * 2
     for s, tiles in ((0, 8), (1, 4)):
         for k in range(tiles):
@@ -1066,10 +1109,15 @@
         block = jnp.where(line == 0, heads, block).astype(BF)
         for d in range(4 * k, 4 * k + 4):
             grad_whole[d // 8, (d // 2) % 4, d % 2, :, 2048:2176] = block
-    behind += [whole_piece(6, 1024, "y"), whole_piece(7, 1536, "x")]
-    drive(*behind)
+    turned_grads(turned, grad_lin, grad_whole, 1024, 4, 1024)
+    p6, p7 = whole_piece(6, 1024, "y"), whole_piece(7, 1536, "x")
+    go(p6, p7)
     final = lk.keep(grad_normed, grad_inputs)
-    drive(line_gather(lk, a_own, a_all, 16))
+    o1 = out_chain()
+    go(o1)
+    go(p4, p5)
+    go(p2, p3)
+    drive(p6, p7, p4, p5, p2, p3, f1, f2, d1, o1)
     final.wait()
     lk.flush()
 
@@ -1080,11 +1128,40 @@
         out_shape=BWD_OUT,
         in_specs=[ANY] * BWD_IN,
         out_specs=[ANY] * len(BWD_OUT),
-        scratch_shapes=sems(128) + BWD_SCRATCH + BWD_WORK + Z_RING * 2 + down_scratch()
+        scratch_shapes=sems(160) + BWD_SCRATCH + BWD_WORK + Z_RING + Z_HALF * 2 + down_scratch()
         + [v for cols in PIECES for v in ring_scratch(cols)],
         compiler_params=pltpu.CompilerParams(
             collective_id=1, has_side_effects=True, vmem_limit_bytes=62 * 2**20
         ),
+    )(*args)
+
+
+def finish_kernel(outputs, grad_inputs, a_all, gu_all, down, *outs):
+    o_out, o_in, o_query, o_key, o_value, o_wout, o_gate, o_up, o_down, o_gains = outs
+    o_out[...] = outputs[...]
+    o_in[...] = grad_inputs[...]
+    for ref, lo, size in (
+        (o_query, 0, 1024), (o_key, 1024, 512), (o_value, 1536, 512), (o_gains, 2048, 128), (o_wout, 2176, 1024),
+    ):
+        total = a_all[0, :, lo : lo + size].astype(F32)
+        for i in range(1, 4):
+            total = total + a_all[i, :, lo : lo + size].astype(F32)
+        ref[...] = total
+    for i in range(4):
+        o_gate[:, 1152 * i : 1152 * i + 1152] = gu_all[i, :, 0:1152].astype(F32)
+        o_up[:, 1152 * i : 1152 * i + 1152] = gu_all[i, :, 1152:2304].astype(F32)
+    o_down[...] = down[...].astype(F32)
+
+
+def finish(*args):
+    return pl.pallas_call(
+        finish_kernel,
+        out_shape=(
+            shape(256, 1024), shape(256, 1024, dtype=F32), shape(32, 1024, dtype=F32), shape(32, 512, dtype=F32),
+            shape(32, 512, dtype=F32), shape(32, 1024, dtype=F32), shape(32, 4608, dtype=F32),
+            shape(32, 4608, dtype=F32), shape(DN, 1024, dtype=F32), shape(32, 128, dtype=F32),
+        ),
+        compiler_params=pltpu.CompilerParams(vmem_limit_bytes=32 * 2**20),
     )(*args)
 
 
@@ -1094,21 +1171,8 @@
 ):
     z = lax.axis_index("seq")
     dp = lax.axis_index("dp")
-    lane = jnp.arange(128)[None, :]
-    line = jnp.arange(32)[:, None]
-
-    def spread(v, row, start):
-        here = jnp.pad(v, (0, 128 - v.shape[0]))
-        return jnp.where(line == row, jnp.roll(here, start)[None, :], 0)
-
-    both = dp % 4 * 32
-    gains = spread(prenorm, 8 + dp // 4, both) + spread(midnorm, 16 + dp // 4, both)
-    for row, v in ((0, querynorm), (1, keynorm)):
-        gains = gains + spread(v, row, 2 * dp) + spread(v, row, 2 * dp + 64)
-    wa = jnp.concatenate([w_query, key_weight, value_weight, gains, w_out], axis=1)
-    gu = jnp.concatenate(
-        [lax.dynamic_slice(w, (0, z * 1152), (32, 1152)) for w in (w_gate, w_up)], axis=1
-    )
+    params = jnp.concatenate([prenorm, midnorm, querynorm, keynorm, jnp.zeros((60,), BF)])
+    params = params.astype(F32).reshape(1, 128)
     pos = z * 128 + jnp.arange(128, dtype=jnp.int32)
     inside = pos - starts[:, 0]
     frequency = ROPE_BASE ** (-(jnp.arange(32, dtype=F32) * 2.0 / 64))
@@ -1120,28 +1184,29 @@
     (
         whole, normed, lin_query, lin_key, keys, values, queries, probs, mixed, middle, gain, grad_gu, grad_down,
         out_part, grad_ffn,
-    ) = forward(wa, gu, w_down, source, upstream, tab, starts[:, 0])
-    outputs, grad_inputs, own_whole, own_gu, own_down, _, _ = backward(
+    ) = forward(
+        w_query, key_weight, value_weight, w_out, w_gate, w_up, w_down, source, upstream, tab, starts[:, 0], params
+    )
+    done = backward(
         whole, normed, lin_query, lin_key, keys, values, queries, probs, mixed, middle, gain, out_part, grad_ffn,
         upstream, source, tab, grad_gu, grad_down,
     )
-    own = jnp.sum(own_whole.astype(F32), axis=0)
-    own_gu = own_gu.astype(F32).transpose(1, 0, 2)
-    grad_gains = own[:, 2048:2176]
+    outputs, grad_inputs, d_query, d_key, d_value, d_out, d_gate, d_up, d_down, d_gains = finish(*done)
+    both = dp % 4 * 32
     return (
         outputs.reshape(2, 1, 128, 1024),
         grad_inputs.reshape(2, 1, 128, 1024),
-        own[:, :1024],
-        own[:, 1024:1536],
-        own[:, 1536:2048],
-        own[:, 2176:],
-        own_gu[:, :, :1152].reshape(32, 4608),
-        own_gu[:, :, 1152:].reshape(32, 4608),
-        own_down.astype(F32),
-        lax.dynamic_slice(grad_gains, (8, both), (1, 32))[0],
-        lax.dynamic_slice(grad_gains, (16, both), (1, 32))[0],
-        lax.dynamic_slice(grad_gains, (0, 2 * dp), (1, 2))[0],
-        lax.dynamic_slice(grad_gains, (0, 64 + 2 * dp), (1, 2))[0],
+        d_query,
+        d_key,
+        d_value,
+        d_out,
+        d_gate,
+        d_up,
+        d_down,
+        lax.dynamic_slice(d_gains, (8, both), (1, 32))[0],
+        lax.dynamic_slice(d_gains, (16, both), (1, 32))[0],
+        lax.dynamic_slice(d_gains, (0, 2 * dp), (1, 2))[0],
+        lax.dynamic_slice(d_gains, (0, 64 + 2 * dp), (1, 2))[0],
     )
 
 

time: 267 us -> 223 us (0.84)
  Pallas kernels: 247 us -> 212 us
  local copies, waits for them, and re-layouts: 13.2 us -> 7.4 us
    pallas_call x1, Pallas kernels: 118 us -> 96.1 us  [backward(): pl.pallas_call(bwd_kernel, out_shape=BWD_OUT, in_specs=[ANY] * BWD_IN, ou...]
    pallas_call x1 -> x2, Pallas kernels: 129 us -> 115 us  [the longest x1 114 us: forward(): pl.pallas_call(fwd_kernel, out_shape=FWD_OUT, in_specs=[ANY] * FWD_IN, ou...]
    unnamed x16 -> x10, local copies, waits for them, and re-layouts: 4.24 us -> 5.43 us
where the time goes in v1:
time: 223 us; the launch traced here: 222 us
  Pallas kernels  212 us (95%)
  local copies, waits for them, and re-layouts  7.4 us (3%)
  other arithmetic  2.58 us (1%)
    pallas_call x1, Pallas kernels, forward(): pl.pallas_call(fwd_kernel, out_shape=FWD_OUT, in_specs=[ANY] * FWD_IN, ou...  114 us
    pallas_call x1, Pallas kernels, backward(): pl.pallas_call(bwd_kernel, out_shape=BWD_OUT, in_specs=[ANY] * BWD_IN, ou...  96.1 us
    unnamed x10, local copies, waits for them, and re-layouts  5.43 us

profile of v1, /device:TPU:0, one launch (start us, length us, event | category | flops | bytes accessed | tf_op | source)
XLA Modules:
  0.0 222.2 jit_solution(9872109220407258837)
XLA Ops:
  0.7 0.7 fusion.1
  1.4 0.5 multiply_cosine_fusion
  1.9 0.8 pad_maximum_fusion.refs_9_.refs_15_
  2.7 0.8 concatenate.26
  3.5 0.5 convert_element_type.19.refs_11_
  4.1 113.5 %shard_map.237 = (bf16[4,4,2,32,3200]{4,3,2,1,0:T(8,128)(2,1)}, bf16[256,1024]{1,0:T(8,128)(2,1)}, f32[256,1024]{1,0:T(8,128)}, f32[256,512]{1,0:T(8,128)}, bf16...) custom-call(bf16[32,1024]{1,0:T(8,128)(2,1)} %refs_0_.1, ...), custom_call_target="tpu_custom_call" | custom-call | tf_op jit(solution)/shard_map/pallas_call | solution.py:818
  117.6 96.1 %shard_map.238 = (bf16[256,1024]{1,0:T(8,128)(2,1)}, f32[256,1024]{1,0:T(8,128)}, bf16[4,32,3200]{2,1,0:T(8,128)(2,1)}, bf16[4,32,2304]{2,1,0:T(8,128)(2,1)}, bf16[144,1024]{1,0:T(8,128)(2,1)}) custom-call(bf16[4,4,2,32,3200]{4,3,2,1,0:T(8,128)(2,1)} %get-tuple-element.43.refs_0_, bf16[256,1024]{1,0:T(8,128)(2,1)} %get-tuple-element.44.refs_1_, ...), custom_call_target="tpu_custom_call" | custom-call | tf_op jit(solution)/shard_map/pallas_call | solution.py:1126
  213.7 0.0 copy-start
  213.7 1.2 copy-done
  214.9 0.0 copy-start.1
  214.9 1.1 copy-done.1
  216.0 0.0 copy-start.2
  216.0 1.1 copy-done.2
  217.1 0.0 copy-start.3
  217.1 1.0 copy-done.3
  218.1 0.0 copy-start.4
  218.1 1.0 copy-done.4
  219.1 1.9 shard_map.239
  221.0 0.6 dynamic-slice_bitcast_fusion
  221.6 0.6 dynamic-slice_bitcast_fusion.2
  (3 shorter events, 0.0 us)
Async XLA Ops:
  213.7 1.2 copy-start
  214.9 1.1 copy-start.1
  216.0 1.1 copy-start.2
  217.1 1.0 copy-start.3
  218.1 1.0 copy-start.4

commit v2 on v1

--- a/solution.py
+++ b/solution.py
@@ -240,8 +240,10 @@
     def part(i, k):
         return out.at[i, pl.ds(0, cut)] if k == 0 else out.at[i, pl.ds(cut, rows - cut)]
 
-    yield from ring_gather(lk, own, lambda i: out.at[i], part, "z", z)
+    rest = ring_gather(lk, own, lambda i: out.at[i], part, "z", z)
+    yield next(rest)
     kept.wait()
+    yield from rest
 
 
 def add_into(dst, src):
@@ -470,48 +472,41 @@
         gain[3:4, pl.ds(128 * k, 128)] = total[1:2]
 
 
-def keys_values(whole, sources, tables, gain, normed, keys, values, lin_key, own):
+def keys_values(q, whole, sources, gain, normed, keys, values, lin_key):
     ones = head_ones()
-
-    def step(q, _):
-        src = sources[q].astype(F32)
-        normed[q] = (src * row_scale(src) * gain[0:1]).astype(BF)
-        cosine, sine = angle_tables(tables[q])
-        kn = gain[3:4, 0:128]
-        lane = lanes_of((256, 128))
-
-        def put(ref, tile, r):
-            turned = pltpu.roll(r, 64, 1)
-            even = jnp.where(lane < 64, r, turned).astype(BF)
-            odd = jnp.where(lane < 64, turned, r).astype(BF)
-            for m in range(2):
-                ref[m, 2 * tile, pl.ds(q * 128, 128)] = even[128 * m : 128 * m + 128]
-                ref[m, 2 * tile + 1, pl.ds(q * 128, 128)] = odd[128 * m : 128 * m + 128]
-
-        for j in range(4):
-            lin = dot(normed[q], flat(whole[:, :, :, :, pl.ds(1024 + 256 * j, 256)]))
-            if j < 2:
-                scale = lax.rsqrt(head_mean(lin * lin, ones) + EPS)
-
-                @pl.when(q == own)
-                def _():
-                    lin_key[:, pl.ds(256 * j, 256)] = lin
-
-                for h in range(2):
-                    cut = slice(128 * h, 128 * h + 128)
-                    v = lin[:, cut] * scale[:, cut] * kn
-                    put(keys, 2 * j + h, v * cosine + halves_swapped(v) * sine)
-            else:
-                for h in range(2):
-                    put(values, 2 * (j - 2) + h, lin[:, 128 * h : 128 * h + 128])
-        return 0
-
-    lax.fori_loop(0, 4, step, 0)
-
-
-def own_queries(whole, tables, gain, normed, lin_query, queries, own):
+    src = sources[q, :, 0:1024].astype(F32)
+    normed[q] = (src * row_scale(src) * gain[0:1]).astype(BF)
+    cosine, sine = angle_tables(sources[q, :, 1024:1152].astype(F32))
+    kn = gain[3:4, 0:128]
+    lane = lanes_of((256, 128))
+    here = pl.ds(pl.multiple_of(q * 128, 128), 128)
+
+    def put(ref, tile, r):
+        turned = pltpu.roll(r, 64, 1)
+        even = jnp.where(lane < 64, r, turned).astype(BF)
+        odd = jnp.where(lane < 64, turned, r).astype(BF)
+        for m in range(2):
+            ref[m, 2 * tile, here] = even[128 * m : 128 * m + 128]
+            ref[m, 2 * tile + 1, here] = odd[128 * m : 128 * m + 128]
+
+    for j in range(4):
+        lin = dot(normed[q], flat(whole[:, :, :, :, pl.ds(1024 + 256 * j, 256)]))
+        if j < 2:
+            scale = lax.rsqrt(head_mean(lin * lin, ones) + EPS)
+            if lin_key is not None:
+                lin_key[:, pl.ds(256 * j, 256)] = lin
+            for h in range(2):
+                cut = slice(128 * h, 128 * h + 128)
+                v = lin[:, cut] * scale[:, cut] * kn
+                put(keys, 2 * j + h, v * cosine + halves_swapped(v) * sine)
+        else:
+            for h in range(2):
+                put(values, 2 * (j - 2) + h, lin[:, 128 * h : 128 * h + 128])
+
+
+def own_queries(whole, table, gain, normed, lin_query, queries, own):
     ones = head_ones()
-    cosine, sine = angle_tables(tables[own])
+    cosine, sine = angle_tables(table[...])
     qn = gain[2:3, 0:128]
     lane = lanes_of((256, 128))
 
@@ -533,18 +528,17 @@
     lax.fori_loop(0, 4, step, 0)
 
 
-def attend(m, queries, keys, values, starts, probs, mixed, own):
+def attend(m, queries, keys, values, starts, mask, probs, mixed, own):
     key_pos = lax.broadcasted_iota(jnp.int32, (512, 256), 0)
     query_pos = own * 128 + lax.broadcasted_iota(jnp.int32, (1, 256), 1) % 128
     lane = lanes_of((128, 128))
-
     row = starts[m : m + 1]
     begin = jnp.concatenate([row, row], axis=1)
+    mask[...] = jnp.where((key_pos <= query_pos) & (key_pos >= begin), 1.0, 0.0)
 
     def step(k, _):
         scores = dot(keys[m, k], queries[m, k], ROWS)
-        scores = jnp.where((key_pos <= query_pos) & (key_pos >= begin), scores, -1e30)
-        raised = jnp.exp(scores - jnp.max(scores, axis=0, keepdims=True))
+        raised = jnp.exp(scores) * mask[...]
         chance = (raised * (1.0 / jnp.sum(raised, axis=0, keepdims=True))).astype(BF)
         probs[8 * m + k] = chance
         got = dot(values[m, k], chance, TOKENS).T
@@ -552,7 +546,10 @@
         mixed[128 * m : 128 * m + 128, pl.ds(pl.multiple_of(k * 128, 128), 128)] = both
         return 0
 
-    lax.fori_loop(0, 8, step, 0)
+    lax.fori_loop(0, 8, step, 0, unroll=UNROLL)
+
+
+UNROLL = 4
 
 
 def out_project(m, whole, sources, gain, mixed, middle, normed_ffn, own):
@@ -585,37 +582,49 @@
     return got.astype(BF)
 
 
-def feed_back_in(cots, down, grad_hidden):
-    def step(i, _):
-        grad_hidden[i] = dot(cots[i], flat(down[...]), ROWS, BF)
-        return 0
-
-    lax.fori_loop(0, 4, step, 0)
-
-
-def feed_chunk(i, ffn, gate_up, down, grad_hidden, hidden, turned, ffn_turned, grad_both, grad_ffn, out_part):
+def feed_back_in(slots, cots, down, grad_hidden):
+    tokens = jnp.concatenate([cots[i] for i in slots], axis=0) if len(slots) > 1 else cots[slots[0]]
+    got = dot(tokens, flat(down[...]), ROWS, BF)
+    for n, i in enumerate(slots):
+        grad_hidden[i] = got[256 * n : 256 * n + 256]
+
+
+def feed_chunk(slots, ffn, gate_up, down, grad_hidden, hidden, turned, ffn_turned, grad_both, grad_ffn, out_part):
+    def load(ref, *cut):
+        return jnp.concatenate([ref[(i, *cut)] for i in slots], axis=0) if len(slots) > 1 else ref[(slots[0], *cut)]
+
+    def store(ref, value, *cut):
+        for n, i in enumerate(slots):
+            ref[(i, *cut)] = value[256 * n : 256 * n + 256]
+
+    every = slice(None)
+    size = 256 * len(slots)
+
     def step(j, _):
         cut = pl.ds(pl.multiple_of(384 * j, 128), 384)
         cut_up = pl.ds(pl.multiple_of(1152 + 384 * j, 128), 384)
-        gated = dot(ffn[i], flat(gate_up[:, :, :, :, cut]))
-        upward = dot(ffn[i], flat(gate_up[:, :, :, :, cut_up]))
+        tokens = load(ffn, every, every)
+        gated = dot(tokens, flat(gate_up[:, :, :, :, cut]))
+        upward = dot(tokens, flat(gate_up[:, :, :, :, cut_up]))
         sigma = 1.0 / (1.0 + jnp.exp(-gated))
         silu = gated * sigma
         made = (silu * upward).astype(BF)
-        hidden[:, cut] = made
-        turned[i, cut] = made.T
-        back = grad_hidden[i, :, cut].astype(F32)
-        grad_both[i, :, cut] = (back * upward * sigma * (1.0 + gated * (1.0 - sigma))).astype(BF)
-        grad_both[i, :, cut_up] = (back * silu).astype(BF)
+        hidden[0:size, cut] = made
+        for n, i in enumerate(slots):
+            turned[cut, pl.ds(pl.multiple_of(256 * i, 256), 256)] = made[256 * n : 256 * n + 256].T
+        back = load(grad_hidden, every, cut).astype(F32)
+        store(grad_both, (back * upward * sigma * (1.0 + gated * (1.0 - sigma))).astype(BF), every, cut)
+        store(grad_both, (back * silu).astype(BF), every, cut_up)
         return 0
 
     lax.fori_loop(0, 3, step, 0)
 
     def last(j, _):
         cut = pl.ds(pl.multiple_of(256 * j, 256), 256)
-        grad_ffn[i, :, cut] = dot(grad_both[i], flat(gate_up[j]), ROWS, BF)
-        out_part[i, :, cut] = dot(hidden[...], flat(down[:, :, :, cut]), kind=BF)
-        ffn_turned[i, cut] = ffn[i, :, cut].T
+        store(grad_ffn, dot(load(grad_both, every, every), flat(gate_up[j]), ROWS, BF), every, cut)
+        store(out_part, dot(hidden[0:size], flat(down[:, :, :, cut]), kind=BF), every, cut)
+        for i in slots:
+            ffn_turned[cut, pl.ds(pl.multiple_of(256 * i, 256), 256)] = ffn[i, :, cut].T
         return 0
 
     lax.fori_loop(0, 4, last, 0)
@@ -624,11 +633,9 @@
 def feed_grads(left, right, out, tiles):
     def step(j, _):
         cut = pl.ds(pl.multiple_of(256 * j, 256), 256)
-        got = dot(left[0], right[0, :, cut])
-        for i in range(1, 4):
-            got = got + dot(left[i], right[i, :, cut])
+        got = dot(left[...], flat(right[:, :, cut]), kind=BF)
         lead = out.shape[:-1]
-        out[(slice(None),) * len(lead) + (cut,)] = got.astype(BF).reshape(*lead, 256)
+        out[(slice(None),) * len(lead) + (cut,)] = got.reshape(*lead, 256)
         return 0
 
     lax.fori_loop(0, tiles, step, 0)
@@ -638,8 +645,9 @@
     pltpu.VMEM((4, 4, 2, 32, WA), BF),
     pltpu.VMEM((4, 4, 2, 32, GU), BF),
     pltpu.VMEM((4, 2, DN, 1024), BF),
-    pltpu.VMEM((4, 256, 1024), BF),
-    pltpu.VMEM((4, 256, 128), F32),
+    pltpu.VMEM((4, 256, 1152), BF),
+    pltpu.VMEM((256, 128), F32),
+    pltpu.VMEM((256, 1152), BF),
     pltpu.VMEM((4, 256, 1024), BF),
     pltpu.VMEM((4, 256, 1024), BF),
     pltpu.VMEM((4, 256, 1024), BF),
@@ -653,20 +661,20 @@
     pltpu.VMEM((256, 1024), F32),
     pltpu.VMEM((8, 1024), F32),
     pltpu.VMEM((4, 256, 1152), BF),
-    pltpu.VMEM((256, 1152), BF),
-    pltpu.VMEM((4, 1152, 256), BF),
-    pltpu.VMEM((4, 1024, 256), BF),
+    pltpu.VMEM((512, 1152), BF),
+    pltpu.VMEM((1152, 1024), BF),
+    pltpu.VMEM((1024, 1024), BF),
     pltpu.VMEM((4, 256, GU), BF),
     pltpu.VMEM((4, 256, 1024), BF),
     pltpu.VMEM((4, 256, 1024), BF),
     pltpu.VMEM((256, 1024), BF),
     pltpu.VMEM((256, 1024), BF),
     pltpu.VMEM((4, 64, 1024), BF),
-    pltpu.VMEM((4, 64, 1024), BF),
     pltpu.VMEM((2, 128), jnp.int32),
     pltpu.VMEM((32, WA), BF),
     pltpu.VMEM((32, GU), BF),
     pltpu.VMEM((1, 128), F32),
+    pltpu.VMEM((512, 256), F32),
 ]
 
 FWD_OUT = (
@@ -702,15 +710,17 @@
     outs, refs = refs[: len(FWD_OUT)], refs[len(FWD_OUT) :]
     lk = Links(*refs[:3])
     (
-        whole, gate_up, down, sources, tables, cots, ffn, normed, lin_query, lin_key, keys, values, queries,
+        whole, gate_up, down, sources, table, source, cots, ffn, normed, lin_query, lin_key, keys, values, queries,
         probs, mixed, middle, gain, grad_hidden, hidden, turned, ffn_turned, grad_both, grad_ffn, out_part,
-        from_right, from_left, passing, from_far, starts, wa, gu, own_params,
+        from_right, from_left, passing, starts, wa, gu, own_params, mask,
     ) = refs[3:]
     own = lk.z
     before, after, far = lk.ring["z"]
     quarter = pl.ds(pl.multiple_of(own * 1152, 128), 1152)
     staged = [
         lk.keep(params_hbm, own_params),
+        lk.keep(tab, table),
+        lk.keep(x, source.at[:, pl.ds(0, 1024)]),
         lk.keep(starts_hbm, starts),
         lk.keep(w_query, wa.at[:, pl.ds(0, 1024)]),
         lk.keep(key_weight, wa.at[:, pl.ds(1024, 512)]),
@@ -720,43 +730,59 @@
         lk.keep(w_up.at[:, quarter], gu.at[:, pl.ds(1152, 1152)]),
     ]
     staged[0].wait()
+    staged[1].wait()
+    source[:, 1024:1152] = table[...].astype(BF)
     wa[:, 2048:2176] = own_gains(own_params[...], lax.axis_index("dp"))
-    for copy in staged[1:]:
+    for copy in staged[2:]:
         copy.wait()
     lk.barrier("xyzc")
-    a1 = plane_gather(lk, wa, whole, "x", 0, 1536)
-    a2 = plane_gather(lk, wa, whole, "y", 1536, WA)
-    t1 = line_gather(lk, tab, tables, 128)
-    x1 = line_gather(lk, x, sources, 128)
+    k1 = plane_gather(lk, wa, whole, "x", 1024, 1536)
+    k2 = plane_gather(lk, wa, whole, "y", 1536, 2176)
+    a1 = plane_gather(lk, wa, whole, "x", 0, 1024)
+    a2 = plane_gather(lk, wa, whole, "y", 2176, WA)
+    x1 = line_gather(lk, source, sources, 128)
     g1 = plane_gather(lk, gu, gate_up, "x", 0, 1152)
     g2 = plane_gather(lk, gu, gate_up, "y", 1152, GU)
     d1 = down_gather(lk, dn, down)
     c1 = line_gather(lk, cot, cots, 128)
-    go(a1, a2, t1, x1)
+    go(k1, k2, x1)
+    go(a1, a2)
+    go(k1, k2)
+    go(a1, a2)
+    go(k1, k2)
+    go(a1, a2)
+    go(k1, k2)
+    go(g1, g2)
+    go(k1, k2)
+    go(a1, a2)
+    go(x1)
+    go(d1)
+    drive(k1, k2)
+    gain_rows(whole, gain)
+    keys_values(own, whole, sources, gain, normed, keys, values, lin_key)
+
+    def sides(i, _):
+        keys_values((own + 3 + 2 * i) % 4, whole, sources, gain, normed, keys, values, None)
+        return 0
+
+    lax.fori_loop(0, 2, sides, 0)
     go(a1, a2)
     go(g1, g2)
-    go(a1, a2)
-    go(t1, x1)
-    go(a1, a2)
+    drive(x1)
+    go(c1)
+    keys_values(far, whole, sources, gain, normed, keys, values, None)
     go(g1, g2)
-    go(a1, a2)
-    go(g1, g2)
+    drive(a1, a2)
+    own_queries(whole, table, gain, normed, lin_query, queries, own)
     go(d1)
-    go(t1, x1)
-    go(c1)
-    drive(a1, a2, t1, x1)
-    gain_rows(whole, gain)
-    saved = [lk.keep(whole, outs[0])]
-    keys_values(whole, sources, tables, gain, normed, keys, values, lin_key, own)
-    go(g1, g2)
-    go(d1)
-    go(c1)
-    own_queries(whole, tables, gain, normed, lin_query, queries, own)
+    saved = []
     for k, ref in enumerate((normed.at[own], lin_query, lin_key, keys, values, queries)):
         saved.append(lk.keep(ref, outs[1 + k]))
     passed = []
     for m in range(2):
-        attend(m, queries, keys, values, starts, probs, mixed, own)
+        attend(m, queries, keys, values, starts, mask, probs, mixed, own)
+        if m == 0:
+            saved.append(lk.keep(whole, outs[0]))
         out_project(m, whole, sources, gain, mixed, middle, ffn, own)
         rows = pl.ds(128 * m, 128)
 
@@ -772,44 +798,63 @@
             go(d1)
             go(c1)
     go(passed[0])
+    go(d1)
+    go(g1, g2)
     for k, ref in enumerate((probs, mixed, middle, gain)):
         saved.append(lk.keep(ref, outs[7 + k]))
-    drive(g1, g2, d1, c1)
-    feed_back_in(cots, down, grad_hidden)
-    go(*passed)
-
-    def chunk(i):
+    drive(g1, g2, d1)
+    feed_back_in((own,), cots, down, grad_hidden)
+    go(passed[1])
+
+    def chunk(*slots):
         feed_chunk(
-            i, ffn, gate_up, down, grad_hidden, hidden, turned, ffn_turned, grad_both, grad_ffn, out_part
+            slots, ffn, gate_up, down, grad_hidden, hidden, turned, ffn_turned, grad_both, grad_ffn, out_part
         )
 
     right, left = lk.sides("z")
     chunk(own)
+    go(c1)
     lk.flush()
-    chunk(before)
-    sent = [lk.put(grad_ffn.at[before], from_right, left)]
-    chunk(after)
-    sent.append(lk.put(grad_ffn.at[after], from_left, right))
-    go(*passed)
+    feed_back_in((before, after), cots, down, grad_hidden)
+    chunk(before, after)
+    low, high = pl.ds(0, 128), pl.ds(128, 128)
+    sent = [
+        lk.put(grad_ffn.at[after, high], from_left.at[high], right),
+        lk.put(grad_ffn.at[before, low], from_right.at[low], left),
+    ]
+    drive(c1)
+    feed_back_in((far,), cots, down, grad_hidden)
+    drive(*passed)
     chunk(far)
     saved.append(lk.keep(out_part, outs[13]))
     hops = []
-    for k in range(4):
-        to = right if k % 2 == 0 else left
-        hops.append((lk.put(grad_ffn.at[far, pl.ds(64 * k, 64)], passing.at[k], to), to))
-    feed_grads(ffn_turned, grad_both, gate_up, 9)
-    saved.append(lk.keep(gate_up, outs[11]))
-    for k, (copy, to) in enumerate(hops):
+    for k in range(2):
+        rows = pl.ds(64 * k, 64)
+        hops.append((lk.put(grad_ffn.at[far, rows], passing.at[k], right), after, rows, from_left, right))
+    for k in range(2):
+        rows = pl.ds(128 + 64 * k, 64)
+        hops.append((lk.put(grad_ffn.at[far, rows], passing.at[2 + k], left), before, rows, from_right, left))
+
+    def hop(k):
+        copy, slot, rows, landing, to = hops[k]
         copy.wait_recv()
-        sent.append(lk.put(passing.at[k], from_far.at[k], to))
+        add_into(grad_ffn.at[slot, rows], passing.at[k])
+        sent.append(lk.put(grad_ffn.at[slot, rows], landing.at[rows], to))
+
     feed_grads(turned, cots, down, 4)
     saved.append(lk.keep(down, outs[12]))
+    hop(0)
+    hop(2)
+    feed_grads(ffn_turned, grad_both, gate_up, 9)
+    hop(1)
+    hop(3)
+    saved.append(lk.keep(gate_up, outs[11]))
     for copy in sent:
         copy.wait_recv()
     for copy in saved:
         copy.wait()
     total = grad_ffn[own].astype(F32) + from_right[...].astype(F32) + from_left[...].astype(F32)
-    lin_query[...] = total + flat(from_far[...]).astype(F32)
+    lin_query[...] = total
     lk.keep(lin_query, outs[14]).wait()
     lk.flush()
 
@@ -820,7 +865,7 @@
         out_shape=FWD_OUT,
         in_specs=[ANY] * FWD_IN,
         out_specs=[ANY] * len(FWD_OUT),
-        scratch_shapes=sems(96) + FWD_SCRATCH,
+        scratch_shapes=sems(128) + FWD_SCRATCH,
         compiler_params=pltpu.CompilerParams(
             collective_id=0, has_side_effects=True, vmem_limit_bytes=60 * 2**20
         ),
@@ -828,7 +873,7 @@
 
 
 BWD_IN = 18
-PIECES = (1152, 1152, 512, 512, 512, 512, 512, 640)
+PIECES = (1152, 1152, 512, 512, 512, 512, 512, 512, 128)
 BWD_OUT = (
     shape(256, 1024),
     shape(256, 1024, dtype=F32),
@@ -939,7 +984,7 @@
 
         return 0
 
-    lax.fori_loop(0, 4, step, 0)
+    lax.fori_loop(0, 4, step, 0, unroll=2)
 
 
 def bwd_kernel(*refs):
@@ -966,9 +1011,9 @@
     outputs, grad_inputs, a_all, gu_all, down_own = outs
     own, c = lk.z, lk.c
 
-    order = [12, 9, 13, 10, 0, 8, 5, 7, 6, 4, 11, 2, 15, 1, 3, 14]
+    order = [11, 12, 9, 13, 10, 0, 8, 5, 7, 6, 4, 2, 15, 1, 3, 14]
     loads = {}
-    for k in order[:6]:
+    for k in order[:7]:
         loads[k] = lk.keep(ins[k], held[k])
     lk.barrier("xyzc")
 
@@ -1005,8 +1050,11 @@
 
     f1, f2 = feed_piece(0, acc_a, 0, "y"), feed_piece(1, acc_b, 1152, "x")
     d1 = down_reduce(lk, grad_down, down_refs, down_own)
-    go(f1, f2, d1)
-    for k in order[6:]:
+    go(d1, f1, f2)
+    o1 = out_chain()
+    need(11)
+    go(o1)
+    for k in order[7:]:
         loads[k] = lk.keep(ins[k], held[k])
     need(12, 9, 13, 10)
     back, row = norm_back(middle[...], gain[1:2], grad_middle[...])
@@ -1015,6 +1063,7 @@
     grad_branch[...] = total.astype(BF)
     gains_back[1:2] = row
     need(0, 8)
+    go(d1)
     lane = lanes_of((256, 128))
 
     def back_mixed(j, _):
@@ -1029,7 +1078,7 @@
         return 0
 
     lax.fori_loop(0, 4, back_mixed, 0)
-    go(f1, f2, d1)
+    go(f2, f1)
     need(5, 7, 6, 4)
     z_kv_m = []
     for m in range(2):
@@ -1043,13 +1092,16 @@
             ring_reduce(lk, lambda i, rows=rows: grad_kv.at[i, rows], part, z_kv[4 * m : 4 * m + 4], "z", own)
         )
         go(z_kv_m[m])
-        go(f1, f2, d1)
+        if m == 0:
+            go(d1)
+            go(f2, f1)
+    go(z_kv_m[0])
     turned[...] = mixed[...].T
     turned_grads(turned, grad_branch, grad_whole, 2176, 4)
     p2, p3 = whole_piece(2, 2176, "y"), whole_piece(3, 2688, "x")
     go(p2, p3)
-    go(*z_kv_m)
-    go(f1, f2, d1)
+    go(d1)
+    go(f2)
     need(2, 15, 1)
     ones = head_ones()
     cosine, sine = angle_tables(table[...])
@@ -1063,16 +1115,22 @@
         return 0
 
     lax.fori_loop(0, 4, back_query, 0)
-    go(p2, p3)
-    go(f1, f2, d1)
+    go(z_kv_m[1])
+    go(d1)
+    go(f2)
     turned[...] = normed[...].T
     turned_grads(turned, grad_lin, grad_whole, 0, 4)
     p4, p5 = whole_piece(4, 0, "y"), whole_piece(5, 512, "x")
     go(p4, p5)
     go(p2, p3)
-    go(f1, f2, d1)
-    need(3, 14, 11)
+    go(f1)
+    go(f2)
+    go(p4, p5)
+    go(p2, p3)
+    go(f1)
+    need(3, 14)
     drive(*z_kv_m)
+    go(o1)
 
     def back_key(j, _):
         cut = pl.ds(pl.multiple_of(256 * j, 256), 256)
@@ -1085,6 +1143,14 @@
     lax.fori_loop(0, 2, back_key, 0)
     grad_lin[:, 1536:2048] = grad_kv[own, :, 512:1024]
 
+    turned_grads(turned, grad_lin, grad_whole, 1024, 4, 1024)
+    p6, p7 = whole_piece(6, 1024, "y"), whole_piece(7, 1536, "x")
+    go(p6, p7)
+    go(d1)
+    go(p2, p3)
+    go(p4, p5)
+    go(f1)
+
     def back_normed(j, _):
         grad_normed[:, pl.ds(pl.multiple_of(256 * j, 256), 256)] = dot(
             grad_lin[...], flat(whole[j, :, :, :, pl.ds(0, 2048)]), ROWS
@@ -1092,9 +1158,14 @@
         return 0
 
     lax.fori_loop(0, 4, back_normed, 0)
+    go(p6, p7)
+    go(p2, p3)
+    go(p4, p5)
+    go(f2, f1)
     back, row = norm_back(source[...].astype(F32), gain[0:1], grad_normed[...])
     gains_back[0:1] = row
     grad_normed[...] = grad_middle[...] + back
+    final = lk.keep(grad_normed, grad_inputs)
     small = [jnp.zeros((1, 128), F32)] * 2
     for s, tiles in ((0, 8), (1, 4)):
         for k in range(tiles):
@@ -1109,15 +1180,27 @@
         block = jnp.where(line == 0, heads, block).astype(BF)
         for d in range(4 * k, 4 * k + 4):
             grad_whole[d // 8, (d // 2) % 4, d % 2, :, 2048:2176] = block
-    turned_grads(turned, grad_lin, grad_whole, 1024, 4, 1024)
-    p6, p7 = whole_piece(6, 1024, "y"), whole_piece(7, 1536, "x")
+    p8 = whole_piece(8, 2048, "y")
+    go(p8)
     go(p6, p7)
-    final = lk.keep(grad_normed, grad_inputs)
-    o1 = out_chain()
-    go(o1)
     go(p4, p5)
+    go(p8)
     go(p2, p3)
-    drive(p6, p7, p4, p5, p2, p3, f1, f2, d1, o1)
+    go(d1)
+    go(p6, p7)
+    go(p8)
+    go(p4, p5)
+    go(f2, f1)
+    go(p6, p7)
+    go(p8)
+    go(p2, p3)
+    go(p6, p7)
+    go(p8)
+    go(p4, p5)
+    go(p6, p7)
+    go(p8)
+    go(d1)
+    drive(p6, p7, p8, p4, p5, p2, p3, f1, f2, o1, d1)
     final.wait()
     lk.flush()
 
@@ -1136,10 +1219,15 @@
     )(*args)
 
 
-def finish_kernel(outputs, grad_inputs, a_all, gu_all, down, *outs):
+def finish_kernel(*refs):
+    ins, outs, held, local = refs[:5], refs[5:15], refs[15:18], refs[18]
     o_out, o_in, o_query, o_key, o_value, o_wout, o_gate, o_up, o_down, o_gains = outs
-    o_out[...] = outputs[...]
-    o_in[...] = grad_inputs[...]
+    a_all, gu_all, down = held
+    pairs = [(ins[2], a_all), (ins[3], gu_all), (ins[4], down), (ins[0], o_out), (ins[1], o_in)]
+    copies = [pltpu.make_async_copy(src, dst, local.at[k]) for k, (src, dst) in enumerate(pairs)]
+    for copy in copies:
+        copy.start()
+    copies[0].wait()
     for ref, lo, size in (
         (o_query, 0, 1024), (o_key, 1024, 512), (o_value, 1536, 512), (o_gains, 2048, 128), (o_wout, 2176, 1024),
     ):
@@ -1147,13 +1235,18 @@
         for i in range(1, 4):
             total = total + a_all[i, :, lo : lo + size].astype(F32)
         ref[...] = total
+    copies[1].wait()
     for i in range(4):
         o_gate[:, 1152 * i : 1152 * i + 1152] = gu_all[i, :, 0:1152].astype(F32)
         o_up[:, 1152 * i : 1152 * i + 1152] = gu_all[i, :, 1152:2304].astype(F32)
+    copies[2].wait()
     o_down[...] = down[...].astype(F32)
+    copies[3].wait()
+    copies[4].wait()
 
 
 def finish(*args):
+    vmem = pl.BlockSpec(memory_space=pltpu.VMEM)
     return pl.pallas_call(
         finish_kernel,
         out_shape=(
@@ -1161,6 +1254,12 @@
             shape(32, 512, dtype=F32), shape(32, 1024, dtype=F32), shape(32, 4608, dtype=F32),
             shape(32, 4608, dtype=F32), shape(DN, 1024, dtype=F32), shape(32, 128, dtype=F32),
         ),
+        in_specs=[ANY] * 5,
+        out_specs=[ANY, ANY] + [vmem] * 8,
+        scratch_shapes=[
+            pltpu.VMEM((4, 32, WA), BF), pltpu.VMEM((4, 32, GU), BF), pltpu.VMEM((DN, 1024), BF),
+            pltpu.SemaphoreType.DMA((5,)),
+        ],
         compiler_params=pltpu.CompilerParams(vmem_limit_bytes=32 * 2**20),
     )(*args)
 

time: 223 us -> 205 us (0.919)
  Pallas kernels: 212 us -> 193 us
    pallas_call x1, Pallas kernels: 96.1 us -> 82.4 us  [backward(): pl.pallas_call(bwd_kernel, out_shape=BWD_OUT, in_specs=[ANY] * BWD_IN, ou...]
    pallas_call x1, Pallas kernels: 114 us -> 108 us  [forward(): pl.pallas_call(fwd_kernel, out_shape=FWD_OUT, in_specs=[ANY] * FWD_IN, ou...]
where the time goes in v2:
time: 205 us; the launch traced here: 204 us
  Pallas kernels  193 us (94%)
  local copies, waits for them, and re-layouts  7.4 us (4%)
  other arithmetic  2.58 us (1%)
    pallas_call x1, Pallas kernels, forward(): pl.pallas_call(fwd_kernel, out_shape=FWD_OUT, in_specs=[ANY] * FWD_IN, ou...  108 us
    pallas_call x1, Pallas kernels, backward(): pl.pallas_call(bwd_kernel, out_shape=BWD_OUT, in_specs=[ANY] * BWD_IN, ou...  82.4 us
    unnamed x10, local copies, waits for them, and re-layouts  5.43 us

profile of v2, /device:TPU:0, one launch (start us, length us, event | category | flops | bytes accessed | tf_op | source)
XLA Modules:
  0.0 204.2 jit_solution(15857685979322485461)
XLA Ops:
  0.7 0.7 fusion.1
  1.4 0.5 multiply_cosine_fusion
  1.9 0.8 pad_maximum_fusion.refs_9_.refs_15_
  2.7 0.8 concatenate.26
  3.5 0.5 convert_element_type.19.refs_11_
  4.1 108.3 %shard_map.237 = (bf16[4,4,2,32,3200]{4,3,2,1,0:T(8,128)(2,1)}, bf16[256,1024]{1,0:T(8,128)(2,1)}, f32[256,1024]{1,0:T(8,128)}, f32[256,512]{1,0:T(8,128)}, bf16...) custom-call(bf16[32,1024]{1,0:T(8,128)(2,1)} %refs_0_.1, ...), custom_call_target="tpu_custom_call" | custom-call | tf_op jit(solution)/shard_map/pallas_call | solution.py:863
  112.4 82.4 %shard_map.238 = (bf16[256,1024]{1,0:T(8,128)(2,1)}, f32[256,1024]{1,0:T(8,128)}, bf16[4,32,3200]{2,1,0:T(8,128)(2,1)}, bf16[4,32,2304]{2,1,0:T(8,128)(2,1)}, bf16[144,1024]{1,0:T(8,128)(2,1)}) custom-call(bf16[4,4,2,32,3200]{4,3,2,1,0:T(8,128)(2,1)} %get-tuple-element.43.refs_0_, bf16[256,1024]{1,0:T(8,128)(2,1)} %get-tuple-element.44.refs_1_, ...), custom_call_target="tpu_custom_call" | custom-call | tf_op jit(solution)/shard_map/pallas_call | solution.py:1209
  194.7 0.0 copy-start
  194.7 1.2 copy-done
  196.0 0.0 copy-start.1
  196.0 1.1 copy-done.1
  197.1 0.0 copy-start.2
  197.1 1.1 copy-done.2
  198.2 0.0 copy-start.3
  198.2 1.0 copy-done.3
  199.2 0.0 copy-start.4
  199.2 1.0 copy-done.4
  200.2 2.8 %shard_map.239 = (bf16[256,1024]{1,0:T(8,128)(2,1)}, f32[256,1024]{1,0:T(8,128)}, f32[32,1024]{1,0:T(8,128)}, f32[32,512]{1,0:T(8,128)}, f32[32,512]{1,0:T(8,128...) custom-call(bf16[256,1024]{1,0:T(8,128)(2,1)S(1)} %copy-done.3, ...), custom_call_target="tpu_custom_call" | custom-call | tf_op jit(solution)/shard_map/pallas_call | solution.py:1250
  203.0 0.6 dynamic-slice_bitcast_fusion
  203.6 0.6 dynamic-slice_bitcast_fusion.2
  (3 shorter events, 0.0 us)
Async XLA Ops:
  194.7 1.2 copy-start
  196.0 1.1 copy-start.1
  197.1 1.1 copy-start.2
  198.2 1.0 copy-start.3
  199.2 1.0 copy-start.4

commit v3 on v2

--- a/solution.py
+++ b/solution.py
@@ -49,14 +49,15 @@
     def sides(self, axis):
         return self.nbr(axis, 1), self.nbr(axis, -1)
 
-    def barrier(self, axes):
+    def barrier(self):
         sem = pltpu.get_barrier_semaphore()
-        count = 0
-        for axis in axes:
-            for step in (1,) if axis == "c" else (1, -1):
-                pl.semaphore_signal(sem, inc=1, device_id=self.nbr(axis, step), device_id_type=MESH)
-                count += 1
-        pl.semaphore_wait(sem, count)
+        targets = [self.nbr(axis, step) for axis in "xy" for step in (1, -1)]
+        for k in range(1, 8):
+            spot = (self.z * 2 + self.c + k) % 8
+            targets.append(self.dev(self.x, self.y, spot % 2, spot // 2))
+        for device in targets:
+            pl.semaphore_signal(sem, inc=1, device_id=device, device_id_type=MESH)
+        pl.semaphore_wait(sem, len(targets))
 
     def make(self, src, dst, to):
         copy = pltpu.make_async_remote_copy(
@@ -246,6 +247,124 @@
     yield from rest
 
 
+def swap_blocks(lk, src, dst, to_row):
+    z, c, n = lk.z, lk.c, lk.n
+    lk.n += 2
+    assert lk.n <= lk.send.shape[0]
+    first = lk.m
+    lk.m += 2
+    copies, keeps, selves = [], [], []
+    for k in range(2):
+        if to_row:
+            slot, core, place = z % 2, z // 2, 2 * k + c
+        else:
+            slot, core, place = z // 2, z % 2, 2 * c + k
+        selves.append((place == z) & (core == c))
+        copies.append(
+            pltpu.make_async_remote_copy(
+                src_ref=src(k),
+                dst_ref=dst(slot),
+                send_sem=lk.send.at[n + k],
+                recv_sem=lk.recv.at[n + slot],
+                device_id=lk.dev(lk.x, lk.y, core, place),
+                device_id_type=MESH,
+            )
+        )
+        keeps.append(pltpu.make_async_copy(src(k), dst(k), lk.local.at[first + k]))
+        pl.when(selves[k])(keeps[k].start)
+        pl.when(jnp.logical_not(selves[k]))(copies[k].start)
+    yield 1
+    for k in range(2):
+        if to_row:
+            own = (z == 2 * c + k) & (c == z % 2)
+        else:
+            own = (z == 2 * k + c) & (c == z // 2)
+        landed = pltpu.make_async_remote_copy(
+            src_ref=src(k),
+            dst_ref=dst(k),
+            send_sem=lk.send.at[n + k],
+            recv_sem=lk.recv.at[n + k],
+            device_id=lk.near["c", 1],
+            device_id_type=MESH,
+        )
+        pl.when(own)(keeps[k].wait)
+        pl.when(jnp.logical_not(own))(landed.wait_recv)
+        pl.when(jnp.logical_not(selves[k]))(copies[k].wait_send)
+
+
+def cots_gather(lk, home, out):
+    z, c = lk.z, lk.c
+    source, place = c == z // 2, (z + 4 - 2 * c) % 4
+    here, there = pl.ds(pl.multiple_of(128 * (z % 2), 128), 128), pl.ds(pl.multiple_of(128 - 128 * (z % 2), 128), 128)
+    over, keeps = [], []
+    for m in range(2):
+        block = home.at[pl.ds(128 * m, 128)]
+        over.append(lk.make(block, out.at[2 * m + c, here], lk.nbr("c", 1)))
+        keeps.append(pltpu.make_async_copy(block, out.at[2 * m + c, here], lk.local.at[lk.m + m]))
+    lk.m += 2
+    right, left = lk.sides("z")
+    own = out.at[:, here]
+    a, b = lk.make(own, own, right), lk.make(own, own, left)
+    half = out.at[pl.ds(0, 2), there]
+    rest = out.at[pl.ds(2, 2), there]
+    e, f = lk.make(half, half, right), lk.make(rest, rest, left)
+    from_left = (place == 1) | (place == 2)
+    from_right = jnp.logical_not(from_left)
+
+    @pl.when(source)
+    def _():
+        for copy in keeps:
+            copy.start()
+
+    @pl.when(jnp.logical_not(source))
+    def _():
+        for copy in over:
+            copy.start()
+
+    yield 1
+
+    @pl.when(source)
+    def _():
+        for copy in keeps:
+            copy.wait()
+        for copy in over:
+            copy.wait_recv()
+        a.start()
+        b.start()
+
+    @pl.when(jnp.logical_not(source))
+    def _():
+        for copy in over:
+            copy.wait_send()
+
+    yield 1
+
+    @pl.when(from_left)
+    def _():
+        a.wait_recv()
+        e.start()
+
+    @pl.when(from_right)
+    def _():
+        b.wait_recv()
+        f.start()
+
+    yield 1
+
+    @pl.when(jnp.logical_not(source))
+    def _():
+        e.wait_recv()
+        f.wait_recv()
+
+    @pl.when(source)
+    def _():
+        a.wait_send()
+        b.wait_send()
+
+    pl.when(from_left)(e.wait_send)
+    pl.when(from_right)(f.wait_send)
+
+
 def add_into(dst, src):
     if len(dst.shape) == 2:
         dst[...] = (dst[...].astype(F32) + src[...].astype(F32)).astype(BF)
@@ -472,29 +591,25 @@
         gain[3:4, pl.ds(128 * k, 128)] = total[1:2]
 
 
-def keys_values(q, whole, sources, gain, normed, keys, values, lin_key):
+def keys_values(whole, source, gain, normed, keys, values, lin_key, core):
     ones = head_ones()
-    src = sources[q, :, 0:1024].astype(F32)
-    normed[q] = (src * row_scale(src) * gain[0:1]).astype(BF)
-    cosine, sine = angle_tables(sources[q, :, 1024:1152].astype(F32))
+    src = source[:, 0:1024].astype(F32)
+    normed[...] = (src * row_scale(src) * gain[0:1]).astype(BF)
+    cosine, sine = angle_tables(source[:, 1024:1152].astype(F32))
     kn = gain[3:4, 0:128]
     lane = lanes_of((256, 128))
-    here = pl.ds(pl.multiple_of(q * 128, 128), 128)
+    here = pl.ds(pl.multiple_of(core * 256, 256), 256)
 
     def put(ref, tile, r):
         turned = pltpu.roll(r, 64, 1)
-        even = jnp.where(lane < 64, r, turned).astype(BF)
-        odd = jnp.where(lane < 64, turned, r).astype(BF)
-        for m in range(2):
-            ref[m, 2 * tile, here] = even[128 * m : 128 * m + 128]
-            ref[m, 2 * tile + 1, here] = odd[128 * m : 128 * m + 128]
+        ref[2 * tile, here] = jnp.where(lane < 64, r, turned).astype(BF)
+        ref[2 * tile + 1, here] = jnp.where(lane < 64, turned, r).astype(BF)
 
     for j in range(4):
-        lin = dot(normed[q], flat(whole[:, :, :, :, pl.ds(1024 + 256 * j, 256)]))
+        lin = dot(normed[...], flat(whole[:, :, :, :, pl.ds(1024 + 256 * j, 256)]))
         if j < 2:
             scale = lax.rsqrt(head_mean(lin * lin, ones) + EPS)
-            if lin_key is not None:
-                lin_key[:, pl.ds(256 * j, 256)] = lin
+            lin_key[:, pl.ds(256 * j, 256)] = lin
             for h in range(2):
                 cut = slice(128 * h, 128 * h + 128)
                 v = lin[:, cut] * scale[:, cut] * kn
@@ -504,14 +619,14 @@
                 put(values, 2 * (j - 2) + h, lin[:, 128 * h : 128 * h + 128])
 
 
-def own_queries(whole, table, gain, normed, lin_query, queries, own):
+def own_queries(whole, source, gain, normed, lin_query, queries):
     ones = head_ones()
-    cosine, sine = angle_tables(table[...])
+    cosine, sine = angle_tables(source[:, 1024:1152].astype(F32))
     qn = gain[2:3, 0:128]
     lane = lanes_of((256, 128))
 
     def step(j, _):
-        lin = dot(normed[own], flat(whole[:, :, :, :, pl.ds(pl.multiple_of(256 * j, 256), 256)]))
+        lin = dot(normed[...], flat(whole[:, :, :, :, pl.ds(pl.multiple_of(256 * j, 256), 256)]))
         lin_query[:, pl.ds(pl.multiple_of(256 * j, 256), 256)] = lin
         scale = lax.rsqrt(head_mean(lin * lin, ones) + EPS)
         for h in range(2):
@@ -528,20 +643,20 @@
     lax.fori_loop(0, 4, step, 0)
 
 
-def attend(m, queries, keys, values, starts, mask, probs, mixed, own):
+def attend(m, queries, keys, values, starts, mask, probs, mixed, core):
     key_pos = lax.broadcasted_iota(jnp.int32, (512, 256), 0)
-    query_pos = own * 128 + lax.broadcasted_iota(jnp.int32, (1, 256), 1) % 128
+    query_pos = core * 256 + 128 * m + lax.broadcasted_iota(jnp.int32, (1, 256), 1) % 128
     lane = lanes_of((128, 128))
-    row = starts[m : m + 1]
+    row = starts[m, 0:1]
     begin = jnp.concatenate([row, row], axis=1)
-    mask[...] = jnp.where((key_pos <= query_pos) & (key_pos >= begin), 1.0, 0.0)
+    mask[...] = jnp.where((key_pos <= query_pos) & (key_pos.astype(F32) >= begin), 1.0, 0.0)
 
     def step(k, _):
-        scores = dot(keys[m, k], queries[m, k], ROWS)
+        scores = dot(keys[k], queries[m, k], ROWS)
         raised = jnp.exp(scores) * mask[...]
         chance = (raised * (1.0 / jnp.sum(raised, axis=0, keepdims=True))).astype(BF)
         probs[8 * m + k] = chance
-        got = dot(values[m, k], chance, TOKENS).T
+        got = dot(values[k], chance, TOKENS).T
         both = jnp.where(lane < 64, got[0:128], got[128:256]).astype(BF)
         mixed[128 * m : 128 * m + 128, pl.ds(pl.multiple_of(k * 128, 128), 128)] = both
         return 0
@@ -552,13 +667,13 @@
 UNROLL = 4
 
 
-def out_project(m, whole, sources, gain, mixed, middle, normed_ffn, own):
+def out_project(m, whole, source, gain, mixed, middle, normed_ffn, own):
     rows = pl.ds(128 * m, 128)
 
     def step(j, _):
         cut = pl.ds(pl.multiple_of(256 * j, 256), 256)
         w = flat(whole[:, :, :, :, pl.ds(pl.multiple_of(2176 + 256 * j, 128), 256)])
-        middle[rows, cut] = sources[own, rows, cut].astype(F32) + dot(mixed[rows], w)
+        middle[rows, cut] = source[rows, cut].astype(F32) + dot(mixed[rows], w)
         return 0
 
     lax.fori_loop(0, 4, step, 0)
@@ -645,16 +760,16 @@
     pltpu.VMEM((4, 4, 2, 32, WA), BF),
     pltpu.VMEM((4, 4, 2, 32, GU), BF),
     pltpu.VMEM((4, 2, DN, 1024), BF),
-    pltpu.VMEM((4, 256, 1152), BF),
+    pltpu.VMEM((256, 1152), BF),
     pltpu.VMEM((256, 128), F32),
     pltpu.VMEM((256, 1152), BF),
     pltpu.VMEM((4, 256, 1024), BF),
     pltpu.VMEM((4, 256, 1024), BF),
-    pltpu.VMEM((4, 256, 1024), BF),
+    pltpu.VMEM((256, 1024), BF),
     pltpu.VMEM((256, 1024), F32),
     pltpu.VMEM((256, 512), F32),
-    pltpu.VMEM((2, 8, 512, 128), BF),
-    pltpu.VMEM((2, 8, 512, 128), BF),
+    pltpu.VMEM((8, 512, 128), BF),
+    pltpu.VMEM((8, 512, 128), BF),
     pltpu.VMEM((2, 8, 256, 128), BF),
     pltpu.VMEM((16, 512, 256), BF),
     pltpu.VMEM((256, 1024), BF),
@@ -670,7 +785,7 @@
     pltpu.VMEM((256, 1024), BF),
     pltpu.VMEM((256, 1024), BF),
     pltpu.VMEM((4, 64, 1024), BF),
-    pltpu.VMEM((2, 128), jnp.int32),
+    pltpu.VMEM((2, 8, 128), F32),
     pltpu.VMEM((32, WA), BF),
     pltpu.VMEM((32, GU), BF),
     pltpu.VMEM((1, 128), F32),
@@ -682,8 +797,8 @@
     shape(256, 1024),
     shape(256, 1024, dtype=F32),
     shape(256, 512, dtype=F32),
-    shape(2, 8, 512, 128),
-    shape(2, 8, 512, 128),
+    shape(8, 512, 128),
+    shape(8, 512, 128),
     shape(2, 8, 256, 128),
     shape(16, 512, 256),
     shape(256, 1024),
@@ -693,6 +808,8 @@
     shape(4, 2, DN, 1024),
     shape(4, 256, 1024),
     shape(256, 1024, dtype=F32),
+    shape(256, 1152),
+    shape(256, 1024),
 )
 
 
@@ -710,7 +827,7 @@
     outs, refs = refs[: len(FWD_OUT)], refs[len(FWD_OUT) :]
     lk = Links(*refs[:3])
     (
-        whole, gate_up, down, sources, table, source, cots, ffn, normed, lin_query, lin_key, keys, values, queries,
+        whole, gate_up, down, source, table, at_home, cots, ffn, normed, lin_query, lin_key, keys, values, queries,
         probs, mixed, middle, gain, grad_hidden, hidden, turned, ffn_turned, grad_both, grad_ffn, out_part,
         from_right, from_left, passing, starts, wa, gu, own_params, mask,
     ) = refs[3:]
@@ -720,8 +837,7 @@
     staged = [
         lk.keep(params_hbm, own_params),
         lk.keep(tab, table),
-        lk.keep(x, source.at[:, pl.ds(0, 1024)]),
-        lk.keep(starts_hbm, starts),
+        lk.keep(x, at_home.at[:, pl.ds(0, 1024)]),
         lk.keep(w_query, wa.at[:, pl.ds(0, 1024)]),
         lk.keep(key_weight, wa.at[:, pl.ds(1024, 512)]),
         lk.keep(value_weight, wa.at[:, pl.ds(1536, 512)]),
@@ -731,59 +847,63 @@
     ]
     staged[0].wait()
     staged[1].wait()
-    source[:, 1024:1152] = table[...].astype(BF)
+    at_home[:, 1024:1152] = table[...].astype(BF)
     wa[:, 2048:2176] = own_gains(own_params[...], lax.axis_index("dp"))
     for copy in staged[2:]:
         copy.wait()
-    lk.barrier("xyzc")
+    lk.barrier()
     k1 = plane_gather(lk, wa, whole, "x", 1024, 1536)
     k2 = plane_gather(lk, wa, whole, "y", 1536, 2176)
     a1 = plane_gather(lk, wa, whole, "x", 0, 1024)
     a2 = plane_gather(lk, wa, whole, "y", 2176, WA)
-    x1 = line_gather(lk, source, sources, 128)
+    half = [pl.ds(0, 128), pl.ds(128, 128)]
+
+    def slot(j):
+        return pl.ds(128 * j, 128) if isinstance(j, int) else pl.ds(pl.multiple_of(128 * j, 128), 128)
+
+    x1 = swap_blocks(lk, lambda m: at_home.at[half[m]], lambda j: source.at[slot(j)], True)
+    s1 = swap_blocks(lk, lambda m: starts_hbm.at[m], lambda j: starts.at[j], True)
     g1 = plane_gather(lk, gu, gate_up, "x", 0, 1152)
     g2 = plane_gather(lk, gu, gate_up, "y", 1152, GU)
     d1 = down_gather(lk, dn, down)
-    c1 = line_gather(lk, cot, cots, 128)
-    go(k1, k2, x1)
+    c1 = cots_gather(lk, cot, cots)
+    go(x1, s1, c1)
+    go(k1, k2)
     go(a1, a2)
     go(k1, k2)
     go(a1, a2)
     go(k1, k2)
     go(a1, a2)
+    go(x1, s1)
+    go(c1)
     go(k1, k2)
     go(g1, g2)
     go(k1, k2)
     go(a1, a2)
-    go(x1)
     go(d1)
-    drive(k1, k2)
+    drive(k1, k2, x1, s1)
     gain_rows(whole, gain)
-    keys_values(own, whole, sources, gain, normed, keys, values, lin_key)
-
-    def sides(i, _):
-        keys_values((own + 3 + 2 * i) % 4, whole, sources, gain, normed, keys, values, None)
-        return 0
-
-    lax.fori_loop(0, 2, sides, 0)
+    keys_values(whole, source, gain, normed, keys, values, lin_key, lk.c)
+    mine = pl.ds(pl.multiple_of(lk.c * 256, 256), 256)
+    crossed = [lk.put(ref.at[:, mine], ref.at[:, mine], lk.nbr("c", 1)) for ref in (keys, values)]
     go(a1, a2)
+    drive(a1, a2)
+    own_queries(whole, source, gain, normed, lin_query, queries)
     go(g1, g2)
-    drive(x1)
     go(c1)
-    keys_values(far, whole, sources, gain, normed, keys, values, None)
-    go(g1, g2)
-    drive(a1, a2)
-    own_queries(whole, table, gain, normed, lin_query, queries, own)
-    go(d1)
-    saved = []
-    for k, ref in enumerate((normed.at[own], lin_query, lin_key, keys, values, queries)):
+    for copy in crossed:
+        copy.wait_recv()
+    saved = [lk.keep(source, outs[15])]
+    for k, ref in enumerate((normed, lin_query, lin_key, keys, values, queries)):
         saved.append(lk.keep(ref, outs[1 + k]))
     passed = []
     for m in range(2):
-        attend(m, queries, keys, values, starts, mask, probs, mixed, own)
+        attend(m, queries, keys, values, starts, mask, probs, mixed, lk.c)
         if m == 0:
+            go(g1, g2)
+            go(d1)
             saved.append(lk.keep(whole, outs[0]))
-        out_project(m, whole, sources, gain, mixed, middle, ffn, own)
+        out_project(m, whole, source, gain, mixed, middle, ffn, own)
         rows = pl.ds(128 * m, 128)
 
         def part(i, k, m=m):
@@ -794,12 +914,14 @@
         )
         go(passed[m])
         if m == 0:
+            go(c1)
             go(g1, g2)
             go(d1)
-            go(c1)
     go(passed[0])
+    go(g1, g2)
     go(d1)
-    go(g1, g2)
+    drive(c1)
+    saved.append(lk.keep(cots.at[own], outs[16]))
     for k, ref in enumerate((probs, mixed, middle, gain)):
         saved.append(lk.keep(ref, outs[7 + k]))
     drive(g1, g2, d1)
@@ -813,7 +935,6 @@
 
     right, left = lk.sides("z")
     chunk(own)
-    go(c1)
     lk.flush()
     feed_back_in((before, after), cots, down, grad_hidden)
     chunk(before, after)
@@ -822,7 +943,6 @@
         lk.put(grad_ffn.at[after, high], from_left.at[high], right),
         lk.put(grad_ffn.at[before, low], from_right.at[low], left),
     ]
-    drive(c1)
     feed_back_in((far,), cots, down, grad_hidden)
     drive(*passed)
     chunk(far)
@@ -872,11 +992,11 @@
     )(*args)
 
 
-BWD_IN = 18
+BWD_IN = 17
 PIECES = (1152, 1152, 512, 512, 512, 512, 512, 512, 128)
 BWD_OUT = (
-    shape(256, 1024),
-    shape(256, 1024, dtype=F32),
+    shape(2, 128, 1024),
+    shape(2, 128, 1024),
     shape(4, 32, WA),
     shape(4, 32, GU),
     shape(DN, 1024),
@@ -886,8 +1006,8 @@
     pltpu.VMEM((256, 1024), BF),
     pltpu.VMEM((256, 1024), F32),
     pltpu.VMEM((256, 512), F32),
-    pltpu.VMEM((2, 8, 512, 128), BF),
-    pltpu.VMEM((2, 8, 512, 128), BF),
+    pltpu.VMEM((8, 512, 128), BF),
+    pltpu.VMEM((8, 512, 128), BF),
     pltpu.VMEM((2, 8, 256, 128), BF),
     pltpu.VMEM((16, 512, 256), BF),
     pltpu.VMEM((256, 1024), BF),
@@ -896,14 +1016,13 @@
     pltpu.VMEM((4, 256, 1024), BF),
     pltpu.VMEM((256, 1024), F32),
     pltpu.VMEM((256, 1024), BF),
-    pltpu.VMEM((256, 1024), BF),
-    pltpu.VMEM((256, 128), F32),
+    pltpu.VMEM((256, 1152), BF),
 ]
 BWD_WORK = [
     pltpu.VMEM((256, 1024), BF),
     pltpu.VMEM((2, 8, 256, 128), BF),
     pltpu.VMEM((256, 1024), F32),
-    pltpu.VMEM((4, 256, 1024), BF),
+    pltpu.VMEM((2, 256, 1024), BF),
     pltpu.VMEM((256, 2048), BF),
     pltpu.VMEM((1024, 256), BF),
     pltpu.VMEM((256, 1024), F32),
@@ -912,18 +1031,14 @@
     pltpu.VMEM((4, 4, 32, 1152), BF),
     pltpu.VMEM((4, 4, 32, 1152), BF),
     pltpu.VMEM((256, 1024), BF),
+    pltpu.VMEM((256, 1024), BF),
+    pltpu.VMEM((256, 1024), BF),
 ]
 Z_RING = [
     pltpu.VMEM((128, 1024), BF),
     pltpu.VMEM((128, 1024), BF),
     pltpu.VMEM((256, 1024), BF),
     pltpu.VMEM((256, 1024), BF),
-]
-Z_HALF = [
-    pltpu.VMEM((64, 1024), BF),
-    pltpu.VMEM((64, 1024), BF),
-    pltpu.VMEM((128, 1024), BF),
-    pltpu.VMEM((128, 1024), BF),
 ]
 
 
@@ -955,7 +1070,7 @@
     lax.fori_loop(0, tiles, step, 0)
 
 
-def attend_back(m, queries, keys, values, probs, grad_mixed, grad_queries, grad_kv):
+def attend_back(queries, keys, values, probs, grad_mixed, grad_queries, grad_kv):
     lane = lanes_of((128, 128))
     lane_keys = lanes_of((512, 128))
 
@@ -963,28 +1078,28 @@
         folded = []
         for e in range(2):
             k = 2 * j + e
-            i = m * 8 + k
-            chance = probs[i]
-            back = dot(values[m, k], grad_mixed[m, k], ROWS)
-            p = chance.astype(F32)
-            p_back = p * back
-            grad_scores = (p_back - p * jnp.sum(p_back, axis=0, keepdims=True)).astype(BF)
-            got = dot(keys[m, k], grad_scores, TOKENS).T
             cut = pl.ds(pl.multiple_of(128 * k, 128), 128)
-            grad_queries[pl.ds(128 * m, 128), cut] = jnp.where(
-                lane < 64, got[0:128], got[128:256]
-            )
-            for v in (dot(grad_scores, queries[m, k]), dot(chance, grad_mixed[m, k])):
-                folded.append(v + pltpu.roll(v, 64, 1))
+            key_sum = value_sum = None
+            for m in range(2):
+                chance = probs[8 * m + k]
+                back = dot(values[k], grad_mixed[m, k], ROWS)
+                p = chance.astype(F32)
+                p_back = p * back
+                grad_scores = (p_back - p * jnp.sum(p_back, axis=0, keepdims=True)).astype(BF)
+                got = dot(keys[k], grad_scores, TOKENS).T
+                grad_queries[128 * m : 128 * m + 128, cut] = jnp.where(lane < 64, got[0:128], got[128:256])
+                more_keys, more_values = dot(grad_scores, queries[m, k]), dot(chance, grad_mixed[m, k])
+                key_sum = more_keys if m == 0 else key_sum + more_keys
+                value_sum = more_values if m == 0 else value_sum + more_values
+            folded += [v + pltpu.roll(v, 64, 1) for v in (key_sum, value_sum)]
         for s in range(2):
             tile = jnp.where(lane_keys < 64, folded[s], folded[2 + s]).astype(BF)
             cut = pl.ds(pl.multiple_of(512 * s + 128 * j, 128), 128)
-            for q in range(4):
-                grad_kv[q, pl.ds(128 * m, 128), cut] = tile[128 * q : 128 * q + 128]
-
+            grad_kv[0, :, cut] = tile[0:256]
+            grad_kv[1, :, cut] = tile[256:512]
         return 0
 
-    lax.fori_loop(0, 4, step, 0, unroll=2)
+    lax.fori_loop(0, 4, step, 0)
 
 
 def bwd_kernel(*refs):
@@ -996,26 +1111,26 @@
     held, refs = refs[:n], refs[n:]
     (
         whole, normed, lin_query, lin_key, keys, values, queries, probs, mixed, middle, gain, out_part, grad_middle,
-        upstream, source, table,
+        upstream, source,
     ) = held
-    grad_gu, grad_down = ins[16:]
+    grad_gu, grad_down = ins[15:]
     n = len(BWD_WORK)
     work, refs = refs[:n], refs[n:]
     (
         grad_branch, grad_mixed, grad_queries, grad_kv, grad_lin, turned, grad_normed, gains_back, grad_whole, acc_a,
-        acc_b, made,
+        acc_b, made, sent_back, kv_other,
     ) = work
-    z_out, z_kv, refs = refs[:4], refs[4:12], refs[12:]
+    z_out, refs = refs[:4], refs[4:]
     down_refs, refs = refs[:10], refs[10:]
     rings = [refs[9 * i : 9 * i + 9] for i in range(len(PIECES))]
     outputs, grad_inputs, a_all, gu_all, down_own = outs
     own, c = lk.z, lk.c
 
-    order = [11, 12, 9, 13, 10, 0, 8, 5, 7, 6, 4, 2, 15, 1, 3, 14]
+    order = [11, 12, 9, 13, 10, 0, 8, 5, 7, 6, 4, 2, 14, 1, 3]
     loads = {}
     for k in order[:7]:
         loads[k] = lk.keep(ins[k], held[k])
-    lk.barrier("xyzc")
+    lk.barrier()
 
     def piece(k, spot, src, out, first, kept=None):
         ring = rings[k]
@@ -1040,9 +1155,9 @@
             lk, lambda i: out_part.at[i], lambda i, k: out_part.at[i, pl.ds(128 * k, 128)], z_out, "z", own
         )
         made[...] = (middle[...] + out_part[own].astype(F32)).astype(BF)
-        done = lk.keep(made, outputs)
-        yield 1
-        done.wait()
+        yield from swap_blocks(
+            lk, lambda j: made.at[pl.ds(128 * j, 128)], lambda m: outputs.at[m], False
+        )
 
     def need(*names):
         for k in names:
@@ -1080,31 +1195,19 @@
     lax.fori_loop(0, 4, back_mixed, 0)
     go(f2, f1)
     need(5, 7, 6, 4)
-    z_kv_m = []
-    for m in range(2):
-        attend_back(m, queries, keys, values, probs, grad_mixed, grad_queries, grad_kv)
-        rows = pl.ds(128 * m, 128)
-
-        def part(i, k, m=m):
-            return grad_kv.at[i, pl.ds(128 * m + 64 * k, 64)]
-
-        z_kv_m.append(
-            ring_reduce(lk, lambda i, rows=rows: grad_kv.at[i, rows], part, z_kv[4 * m : 4 * m + 4], "z", own)
-        )
-        go(z_kv_m[m])
-        if m == 0:
-            go(d1)
-            go(f2, f1)
-    go(z_kv_m[0])
+    attend_back(queries, keys, values, probs, grad_mixed, grad_queries, grad_kv)
+    crossed = lk.put(grad_kv.at[lk.other], kv_other, lk.nbr("c", 1))
+    go(d1)
+    go(f2, f1)
     turned[...] = mixed[...].T
     turned_grads(turned, grad_branch, grad_whole, 2176, 4)
     p2, p3 = whole_piece(2, 2176, "y"), whole_piece(3, 2688, "x")
     go(p2, p3)
     go(d1)
     go(f2)
-    need(2, 15, 1)
+    need(2, 14, 1)
     ones = head_ones()
-    cosine, sine = angle_tables(table[...])
+    cosine, sine = angle_tables(source[:, 1024:1152].astype(F32))
 
     def back_query(j, _):
         cut = pl.ds(pl.multiple_of(256 * j, 256), 256)
@@ -1115,41 +1218,32 @@
         return 0
 
     lax.fori_loop(0, 4, back_query, 0)
-    go(z_kv_m[1])
+    turned[...] = normed[...].T
+    need(3)
+    crossed.wait_recv()
+
+    def back_key(j, _):
+        cut = pl.ds(pl.multiple_of(256 * j, 256), 256)
+        grad = grad_kv[c, :, cut].astype(F32) + kv_other[:, cut].astype(F32)
+        got, line = heads_back(lin_key[:, cut], grad, gain[3:4, 0:256], cosine, sine, ones)
+        grad_lin[:, pl.ds(pl.multiple_of(1024 + 256 * j, 256), 256)] = got.astype(BF)
+        gains_back[3:4, cut] = line
+        return 0
+
+    lax.fori_loop(0, 2, back_key, 0)
+    value_sum = grad_kv[c, :, 512:1024].astype(F32) + kv_other[:, 512:1024].astype(F32)
+    grad_lin[:, 1536:2048] = value_sum.astype(BF)
+
+    turned_grads(turned, grad_lin, grad_whole, 1024, 4, 1024)
+    p6, p7 = whole_piece(6, 1024, "y"), whole_piece(7, 1536, "x")
+    go(p6, p7)
     go(d1)
     go(f2)
-    turned[...] = normed[...].T
     turned_grads(turned, grad_lin, grad_whole, 0, 4)
     p4, p5 = whole_piece(4, 0, "y"), whole_piece(5, 512, "x")
     go(p4, p5)
     go(p2, p3)
     go(f1)
-    go(f2)
-    go(p4, p5)
-    go(p2, p3)
-    go(f1)
-    need(3, 14)
-    drive(*z_kv_m)
-    go(o1)
-
-    def back_key(j, _):
-        cut = pl.ds(pl.multiple_of(256 * j, 256), 256)
-        grad = grad_kv[own, :, cut].astype(F32)
-        got, line = heads_back(lin_key[:, cut], grad, gain[3:4, 0:256], cosine, sine, ones)
-        grad_lin[:, pl.ds(pl.multiple_of(1024 + 256 * j, 256), 256)] = got.astype(BF)
-        gains_back[3:4, cut] = line
-        return 0
-
-    lax.fori_loop(0, 2, back_key, 0)
-    grad_lin[:, 1536:2048] = grad_kv[own, :, 512:1024]
-
-    turned_grads(turned, grad_lin, grad_whole, 1024, 4, 1024)
-    p6, p7 = whole_piece(6, 1024, "y"), whole_piece(7, 1536, "x")
-    go(p6, p7)
-    go(d1)
-    go(p2, p3)
-    go(p4, p5)
-    go(f1)
 
     def back_normed(j, _):
         grad_normed[:, pl.ds(pl.multiple_of(256 * j, 256), 256)] = dot(
@@ -1160,12 +1254,13 @@
     lax.fori_loop(0, 4, back_normed, 0)
     go(p6, p7)
     go(p2, p3)
-    go(p4, p5)
+    go(o1)
     go(f2, f1)
-    back, row = norm_back(source[...].astype(F32), gain[0:1], grad_normed[...])
+    back, row = norm_back(source[:, 0:1024].astype(F32), gain[0:1], grad_normed[...])
     gains_back[0:1] = row
-    grad_normed[...] = grad_middle[...] + back
-    final = lk.keep(grad_normed, grad_inputs)
+    sent_back[...] = (grad_middle[...] + back).astype(BF)
+    i1 = swap_blocks(lk, lambda j: sent_back.at[pl.ds(128 * j, 128)], lambda m: grad_inputs.at[m], False)
+    go(i1)
     small = [jnp.zeros((1, 128), F32)] * 2
     for s, tiles in ((0, 8), (1, 4)):
         for k in range(tiles):
@@ -1182,26 +1277,30 @@
             grad_whole[d // 8, (d // 2) % 4, d % 2, :, 2048:2176] = block
     p8 = whole_piece(8, 2048, "y")
     go(p8)
+    go(p4, p5)
+    go(p6, p7)
+    go(p2, p3)
+    go(d1)
+    go(p8)
+    go(p4, p5)
+    go(p6, p7)
+    go(f2, f1)
+    go(p2, p3)
+    go(p8)
+    go(d1)
+    go(p4, p5)
+    go(p6, p7)
+    go(o1)
+    go(p8)
+    go(f2, f1)
+    go(p2, p3)
     go(p6, p7)
     go(p4, p5)
     go(p8)
-    go(p2, p3)
-    go(d1)
     go(p6, p7)
+    go(p4, p5)
     go(p8)
-    go(p4, p5)
-    go(f2, f1)
-    go(p6, p7)
-    go(p8)
-    go(p2, p3)
-    go(p6, p7)
-    go(p8)
-    go(p4, p5)
-    go(p6, p7)
-    go(p8)
-    go(d1)
-    drive(p6, p7, p8, p4, p5, p2, p3, f1, f2, o1, d1)
-    final.wait()
+    drive(p6, p7, p4, p5, p8, p2, p3, f1, f2, d1, o1, i1)
     lk.flush()
 
 
@@ -1211,7 +1310,7 @@
         out_shape=BWD_OUT,
         in_specs=[ANY] * BWD_IN,
         out_specs=[ANY] * len(BWD_OUT),
-        scratch_shapes=sems(160) + BWD_SCRATCH + BWD_WORK + Z_RING + Z_HALF * 2 + down_scratch()
+        scratch_shapes=sems(160) + BWD_SCRATCH + BWD_WORK + Z_RING + down_scratch()
         + [v for cols in PIECES for v in ring_scratch(cols)],
         compiler_params=pltpu.CompilerParams(
             collective_id=1, has_side_effects=True, vmem_limit_bytes=62 * 2**20
@@ -1220,10 +1319,10 @@
 
 
 def finish_kernel(*refs):
-    ins, outs, held, local = refs[:5], refs[5:15], refs[15:18], refs[18]
+    ins, outs, held, local = refs[:5], refs[5:15], refs[15:19], refs[19]
     o_out, o_in, o_query, o_key, o_value, o_wout, o_gate, o_up, o_down, o_gains = outs
-    a_all, gu_all, down = held
-    pairs = [(ins[2], a_all), (ins[3], gu_all), (ins[4], down), (ins[0], o_out), (ins[1], o_in)]
+    a_all, gu_all, down, grad_in = held
+    pairs = [(ins[2], a_all), (ins[3], gu_all), (ins[4], down), (ins[0], o_out), (ins[1], grad_in)]
     copies = [pltpu.make_async_copy(src, dst, local.at[k]) for k, (src, dst) in enumerate(pairs)]
     for copy in copies:
         copy.start()
@@ -1241,8 +1340,9 @@
         o_up[:, 1152 * i : 1152 * i + 1152] = gu_all[i, :, 1152:2304].astype(F32)
     copies[2].wait()
     o_down[...] = down[...].astype(F32)
+    copies[4].wait()
+    o_in[...] = grad_in[...].astype(F32)
     copies[3].wait()
-    copies[4].wait()
 
 
 def finish(*args):
@@ -1250,17 +1350,17 @@
     return pl.pallas_call(
         finish_kernel,
         out_shape=(
-            shape(256, 1024), shape(256, 1024, dtype=F32), shape(32, 1024, dtype=F32), shape(32, 512, dtype=F32),
+            shape(2, 128, 1024), shape(2, 128, 1024, dtype=F32), shape(32, 1024, dtype=F32), shape(32, 512, dtype=F32),
             shape(32, 512, dtype=F32), shape(32, 1024, dtype=F32), shape(32, 4608, dtype=F32),
             shape(32, 4608, dtype=F32), shape(DN, 1024, dtype=F32), shape(32, 128, dtype=F32),
         ),
         in_specs=[ANY] * 5,
-        out_specs=[ANY, ANY] + [vmem] * 8,
+        out_specs=[ANY] + [vmem] * 9,
         scratch_shapes=[
             pltpu.VMEM((4, 32, WA), BF), pltpu.VMEM((4, 32, GU), BF), pltpu.VMEM((DN, 1024), BF),
-            pltpu.SemaphoreType.DMA((5,)),
+            pltpu.VMEM((2, 128, 1024), BF), pltpu.SemaphoreType.DMA((5,)),
         ],
-        compiler_params=pltpu.CompilerParams(vmem_limit_bytes=32 * 2**20),
+        compiler_params=pltpu.CompilerParams(vmem_limit_bytes=60 * 2**20),
     )(*args)
 
 
@@ -1278,17 +1378,18 @@
     angle = inside.reshape(256, 1).astype(F32) * frequency[None, :]
     cosine, sine = jnp.cos(angle), jnp.sin(angle)
     tab = jnp.concatenate([cosine, cosine, -sine, sine], axis=1)
+    begin = jnp.broadcast_to(starts.astype(F32), (2, 8, 128))
     source = inputs.reshape(256, 1024)
     upstream = cotangent.reshape(256, 1024)
     (
         whole, normed, lin_query, lin_key, keys, values, queries, probs, mixed, middle, gain, grad_gu, grad_down,
-        out_part, grad_ffn,
+        out_part, grad_ffn, row_source, row_upstream,
     ) = forward(
-        w_query, key_weight, value_weight, w_out, w_gate, w_up, w_down, source, upstream, tab, starts[:, 0], params
+        w_query, key_weight, value_weight, w_out, w_gate, w_up, w_down, source, upstream, tab, begin, params
     )
     done = backward(
         whole, normed, lin_query, lin_key, keys, values, queries, probs, mixed, middle, gain, out_part, grad_ffn,
-        upstream, source, tab, grad_gu, grad_down,
+        row_upstream, row_source, grad_gu, grad_down,
     )
     outputs, grad_inputs, d_query, d_key, d_value, d_out, d_gate, d_up, d_down, d_gains = finish(*done)
     both = dp % 4 * 32

time: 205 us -> 234 us (1.14)
  Pallas kernels: 193 us -> 225 us
  local copies, waits for them, and re-layouts: 7.4 us -> 4.02 us
    pallas_call x1, Pallas kernels: 2.79 us -> 18.7 us  [finish(): pl.pallas_call(finish_kernel, out_shape=(shape(2, 128, 1024), shape(2, 12...]
    pallas_call x1, Pallas kernels: 82.4 us -> 98.2 us  [backward(): pl.pallas_call(bwd_kernel, out_shape=BWD_OUT, in_specs=[ANY] * BWD_IN, ou...]
    unnamed x10 -> x0, local copies, waits for them, and re-layouts: 5.43 us -> none
where the time goes in v3:
time: 234 us; the launch traced here: 233 us
  Pallas kernels  225 us (96%)
  local copies, waits for them, and re-layouts  4.02 us (2%)
  other arithmetic  3.26 us (1%)
    pallas_call x1, Pallas kernels, forward(): pl.pallas_call(fwd_kernel, out_shape=FWD_OUT, in_specs=[ANY] * FWD_IN, ou...  108 us
    pallas_call x1, Pallas kernels, backward(): pl.pallas_call(bwd_kernel, out_shape=BWD_OUT, in_specs=[ANY] * BWD_IN, ou...  98.2 us
    pallas_call x1, Pallas kernels, finish(): pl.pallas_call(finish_kernel, out_shape=(shape(2, 128, 1024), shape(2, 12...  18.7 us

profile of v3, /device:TPU:0, one launch (start us, length us, event | category | flops | bytes accessed | tf_op | source)
XLA Modules:
  0.0 233.4 jit_solution(17467826501355362026)
XLA Ops:
  0.7 0.7 fusion.1
  1.4 0.5 multiply_cosine_fusion
  1.9 0.8 pad_maximum_fusion.refs_9_
  2.7 0.7 convert_element_type.22
  3.4 0.6 broadcast_in_dim.13.refs_10_
  4.0 0.8 concatenate.26
  4.8 0.5 convert_element_type.23.refs_11_
  5.3 108.5 %shard_map.237 = (bf16[4,4,2,32,3200]{4,3,2,1,0:T(8,128)(2,1)}, bf16[256,1024]{1,0:T(8,128)(2,1)}, f32[256,1024]{1,0:T(8,128)}, f32[256,512]{1,0:T(8,128)}, bf16...) custom-call(bf16[32,1024]{1,0:T(8,128)(2,1)} %refs_0_.1, ...), custom_call_target="tpu_custom_call" | custom-call | tf_op jit(solution)/shard_map/pallas_call | solution.py:983
  113.8 98.2 %shard_map.238 = (bf16[2,128,1024]{2,1,0:T(8,128)(2,1)}, bf16[2,128,1024]{2,1,0:T(8,128)(2,1)}, bf16[4,32,3200]{2,1,0:T(8,128)(2,1)}, bf16[4,32,2304]{2,1,0:T(8,128)(2,1)}, bf16[144,1024]{1,0:T(8,128)(2,1)}) custom-call(bf16[4,4,2,32,3200]{4,3,2,1,0:T(8,128)(2,1)} %get-tuple-element.45.refs_0_, bf16[256,1024]{1,0:T(8,128)(2,1)} %get-tuple-element.46.refs_1_, ...), custom_call_target="tpu_custom_call" | custom-call | tf_op jit(solution)/shard_map/pallas_call | solution.py:1308
  212.0 18.7 %shard_map.239 = (bf16[2,128,1024]{2,1,0:T(8,128)(2,1)}, f32[2,128,1024]{2,1,0:T(8,128)}, f32[32,1024]{1,0:T(8,128)}, f32[32,512]{1,0:T(8,128)}, f32[32,512]{1,0...) custom-call(bf16[2,128,1024]{2,1,0:T(8,128)(2,1)} %get-tuple-element, ...), custom_call_target="tpu_custom_call" | custom-call | tf_op jit(solution)/shard_map/pallas_call | solution.py:1350
  230.8 1.3 dynamic-slice_bitcast_fusion
  232.1 1.3 dynamic-slice_bitcast_fusion.2
  (3 shorter events, 0.0 us)

commit v4 on v3

--- a/solution.py
+++ b/solution.py
@@ -211,23 +211,26 @@
         d.wait_send()
 
 
-def down_part(k):
-    return pl.ds(0, 80) if k == 0 else pl.ds(80, 64)
-
-
-def down_gather(lk, own, out):
+def down_cut(lo, rows):
+    first = (rows // 16 + 1) // 2 * 16
+    return lambda k: pl.ds(lo, first) if k == 0 else pl.ds(lo + first, rows - first)
+
+
+def down_gather(lk, own, out, lo, rows):
     y, c = lk.y, lk.c
+    every, cut = pl.ds(lo, rows), down_cut(lo, rows)
     yield from ring_spread(
-        lk, own, out.at[y, c], lambda k: out.at[y, c, down_part(k)], "x", lk.past_x
+        lk, own.at[every], out.at[y, c, every], lambda k: out.at[y, c, cut(k)], "x", lk.past_x
     )
     crossing = []
 
     def cross(j):
-        crossing.append(lk.put(out.at[j, c], out.at[j, c], lk.nbr("c", 1)))
+        ref = out.at[j, c, every]
+        crossing.append(lk.put(ref, ref, lk.nbr("c", 1)))
 
     cross(y)
     yield from ring_gather(
-        lk, out.at[y, c], lambda j: out.at[j, c], lambda j, k: out.at[j, c, down_part(k)], "y", y, cross
+        lk, out.at[y, c, every], lambda j: out.at[j, c, every], lambda j, k: out.at[j, c, cut(k)], "y", y, cross
     )
     yield 1
     for copy in crossing:
@@ -440,26 +443,18 @@
     ]
 
 
-def down_scratch():
-    return [
-        pltpu.VMEM((4, DN, 1024), BF),
-        pltpu.VMEM((4, DN, 1024), BF),
-        pltpu.VMEM((80, 1024), BF),
-        pltpu.VMEM((64, 1024), BF),
-        pltpu.VMEM((DN, 1024), BF),
-        pltpu.VMEM((DN, 1024), BF),
-        pltpu.VMEM((80, 1024), BF),
-        pltpu.VMEM((64, 1024), BF),
-        pltpu.VMEM((DN, 1024), BF),
-        pltpu.VMEM((DN, 1024), BF),
-    ]
-
-
-def down_reduce(lk, part_hbm, s, out):
+def down_scratch(rows):
+    first = (rows // 16 + 1) // 2 * 16
+    ring = [(first, 1024), (rows - first, 1024), (rows, 1024), (rows, 1024)]
+    return [pltpu.VMEM(dims, BF) for dims in [(4, rows, 1024)] * 2 + ring * 2]
+
+
+def down_reduce(lk, part_hbm, s, out, lo, rows):
     acc, sib, one, (x0, x1, xa, xb) = s[0], s[1], s[2:6], s[6:10]
     y, c = lk.y, lk.c
-    kept = lk.keep(part_hbm.at[:, c], acc)
-    got = lk.put(part_hbm.at[:, 1 - c], sib, lk.nbr("c", 1))
+    every, cut, down_part = pl.ds(lo, rows), down_cut(lo, rows), down_cut(0, rows)
+    kept = lk.keep(part_hbm.at[:, c, every], acc)
+    got = lk.put(part_hbm.at[:, lk.other, every], sib, lk.nbr("c", 1))
     yield 1
     kept.wait()
     got.wait_recv()
@@ -517,7 +512,7 @@
         b.wait_send()
 
     yield from ring_spread(
-        lk, mine, out, lambda k: out.at[down_part(k)], "z", lk.past_z
+        lk, mine, out.at[every], lambda k: out.at[cut(k)], "z", lk.past_z
     )
 
 
@@ -865,7 +860,7 @@
     s1 = swap_blocks(lk, lambda m: starts_hbm.at[m], lambda j: starts.at[j], True)
     g1 = plane_gather(lk, gu, gate_up, "x", 0, 1152)
     g2 = plane_gather(lk, gu, gate_up, "y", 1152, GU)
-    d1 = down_gather(lk, dn, down)
+    d1, d2 = down_gather(lk, dn, down, 0, 80), down_gather(lk, dn, down, 80, 64)
     c1 = cots_gather(lk, cot, cots)
     go(x1, s1, c1)
     go(k1, k2)
@@ -880,16 +875,17 @@
     go(g1, g2)
     go(k1, k2)
     go(a1, a2)
-    go(d1)
+    go(d1, d2)
     drive(k1, k2, x1, s1)
     gain_rows(whole, gain)
     keys_values(whole, source, gain, normed, keys, values, lin_key, lk.c)
     mine = pl.ds(pl.multiple_of(lk.c * 256, 256), 256)
     crossed = [lk.put(ref.at[:, mine], ref.at[:, mine], lk.nbr("c", 1)) for ref in (keys, values)]
-    go(a1, a2)
+    go(g1, g2)
     drive(a1, a2)
+    go(g1, g2)
     own_queries(whole, source, gain, normed, lin_query, queries)
-    go(g1, g2)
+    go(d1, d2)
     go(c1)
     for copy in crossed:
         copy.wait_recv()
@@ -899,9 +895,9 @@
     passed = []
     for m in range(2):
         attend(m, queries, keys, values, starts, mask, probs, mixed, lk.c)
+        go(g1, g2)
         if m == 0:
-            go(g1, g2)
-            go(d1)
+            go(d1, d2)
             saved.append(lk.keep(whole, outs[0]))
         out_project(m, whole, source, gain, mixed, middle, ffn, own)
         rows = pl.ds(128 * m, 128)
@@ -915,18 +911,14 @@
         go(passed[m])
         if m == 0:
             go(c1)
-            go(g1, g2)
-            go(d1)
     go(passed[0])
-    go(g1, g2)
-    go(d1)
+    go(d1, d2)
     drive(c1)
     saved.append(lk.keep(cots.at[own], outs[16]))
     for k, ref in enumerate((probs, mixed, middle, gain)):
         saved.append(lk.keep(ref, outs[7 + k]))
-    drive(g1, g2, d1)
+    drive(g1, g2, d1, d2)
     feed_back_in((own,), cots, down, grad_hidden)
-    go(passed[1])
 
     def chunk(*slots):
         feed_chunk(
@@ -935,7 +927,7 @@
 
     right, left = lk.sides("z")
     chunk(own)
-    lk.flush()
+    go(passed[1])
     feed_back_in((before, after), cots, down, grad_hidden)
     chunk(before, after)
     low, high = pl.ds(0, 128), pl.ds(128, 128)
@@ -946,6 +938,7 @@
     feed_back_in((far,), cots, down, grad_hidden)
     drive(*passed)
     chunk(far)
+    lk.flush()
     saved.append(lk.keep(out_part, outs[13]))
     hops = []
     for k in range(2):
@@ -985,7 +978,7 @@
         out_shape=FWD_OUT,
         in_specs=[ANY] * FWD_IN,
         out_specs=[ANY] * len(FWD_OUT),
-        scratch_shapes=sems(128) + FWD_SCRATCH,
+        scratch_shapes=sems(160) + FWD_SCRATCH,
         compiler_params=pltpu.CompilerParams(
             collective_id=0, has_side_effects=True, vmem_limit_bytes=60 * 2**20
         ),
@@ -1070,7 +1063,7 @@
     lax.fori_loop(0, tiles, step, 0)
 
 
-def attend_back(queries, keys, values, probs, grad_mixed, grad_queries, grad_kv):
+def attend_back(half, queries, keys, values, probs, grad_mixed, grad_queries, grad_kv):
     lane = lanes_of((128, 128))
     lane_keys = lanes_of((512, 128))
 
@@ -1099,7 +1092,7 @@
             grad_kv[1, :, cut] = tile[256:512]
         return 0
 
-    lax.fori_loop(0, 4, step, 0)
+    lax.fori_loop(2 * half, 2 * half + 2, step, 0)
 
 
 def bwd_kernel(*refs):
@@ -1121,7 +1114,7 @@
         acc_b, made, sent_back, kv_other,
     ) = work
     z_out, refs = refs[:4], refs[4:]
-    down_refs, refs = refs[:10], refs[10:]
+    down_refs, refs = refs[:20], refs[20:]
     rings = [refs[9 * i : 9 * i + 9] for i in range(len(PIECES))]
     outputs, grad_inputs, a_all, gu_all, down_own = outs
     own, c = lk.z, lk.c
@@ -1164,8 +1157,9 @@
             loads.pop(k).wait()
 
     f1, f2 = feed_piece(0, acc_a, 0, "y"), feed_piece(1, acc_b, 1152, "x")
-    d1 = down_reduce(lk, grad_down, down_refs, down_own)
-    go(d1, f1, f2)
+    d1 = down_reduce(lk, grad_down, down_refs[:10], down_own, 0, 80)
+    d2 = down_reduce(lk, grad_down, down_refs[10:], down_own, 80, 64)
+    go(d1, d2, f1, f2)
     o1 = out_chain()
     need(11)
     go(o1)
@@ -1178,7 +1172,7 @@
     grad_branch[...] = total.astype(BF)
     gains_back[1:2] = row
     need(0, 8)
-    go(d1)
+    go(d1, d2)
     lane = lanes_of((256, 128))
 
     def back_mixed(j, _):
@@ -1195,15 +1189,17 @@
     lax.fori_loop(0, 4, back_mixed, 0)
     go(f2, f1)
     need(5, 7, 6, 4)
-    attend_back(queries, keys, values, probs, grad_mixed, grad_queries, grad_kv)
+    attend_back(0, queries, keys, values, probs, grad_mixed, grad_queries, grad_kv)
+    go(d1, d2)
+    go(f2, f1)
+    go(o1)
+    attend_back(1, queries, keys, values, probs, grad_mixed, grad_queries, grad_kv)
     crossed = lk.put(grad_kv.at[lk.other], kv_other, lk.nbr("c", 1))
-    go(d1)
-    go(f2, f1)
     turned[...] = mixed[...].T
     turned_grads(turned, grad_branch, grad_whole, 2176, 4)
     p2, p3 = whole_piece(2, 2176, "y"), whole_piece(3, 2688, "x")
     go(p2, p3)
-    go(d1)
+    go(d1, d2)
     go(f2)
     need(2, 14, 1)
     ones = head_ones()
@@ -1237,13 +1233,15 @@
     turned_grads(turned, grad_lin, grad_whole, 1024, 4, 1024)
     p6, p7 = whole_piece(6, 1024, "y"), whole_piece(7, 1536, "x")
     go(p6, p7)
-    go(d1)
-    go(f2)
+    go(d1, d2)
+    go(f1, f2)
+    go(p2, p3)
     turned_grads(turned, grad_lin, grad_whole, 0, 4)
+    go(o1)
     p4, p5 = whole_piece(4, 0, "y"), whole_piece(5, 512, "x")
     go(p4, p5)
-    go(p2, p3)
-    go(f1)
+    go(p6, p7)
+    go(d1, d2)
 
     def back_normed(j, _):
         grad_normed[:, pl.ds(pl.multiple_of(256 * j, 256), 256)] = dot(
@@ -1252,10 +1250,11 @@
         return 0
 
     lax.fori_loop(0, 4, back_normed, 0)
+    go(p2, p3)
     go(p6, p7)
-    go(p2, p3)
-    go(o1)
+    go(p4, p5)
     go(f2, f1)
+    go(d1, d2)
     back, row = norm_back(source[:, 0:1024].astype(F32), gain[0:1], grad_normed[...])
     gains_back[0:1] = row
     sent_back[...] = (grad_middle[...] + back).astype(BF)
@@ -1277,30 +1276,30 @@
             grad_whole[d // 8, (d // 2) % 4, d % 2, :, 2048:2176] = block
     p8 = whole_piece(8, 2048, "y")
     go(p8)
+    go(p2, p3)
+    go(p6, p7)
     go(p4, p5)
+    go(p8)
+    go(d1, d2)
+    go(p2, p3)
     go(p6, p7)
-    go(p2, p3)
-    go(d1)
-    go(p8)
     go(p4, p5)
-    go(p6, p7)
-    go(f2, f1)
-    go(p2, p3)
-    go(p8)
-    go(d1)
-    go(p4, p5)
-    go(p6, p7)
-    go(o1)
     go(p8)
     go(f2, f1)
     go(p2, p3)
     go(p6, p7)
     go(p4, p5)
     go(p8)
+    go(d1, d2)
+    go(o1)
+    go(p2, p3)
     go(p6, p7)
     go(p4, p5)
     go(p8)
-    drive(p6, p7, p4, p5, p8, p2, p3, f1, f2, d1, o1, i1)
+    go(i1)
+    go(f2, f1)
+    go(d1, d2)
+    drive(p6, p7, p4, p5, p8, p2, p3, f1, f2, d1, d2, o1, i1)
     lk.flush()
 
 
@@ -1310,7 +1309,7 @@
         out_shape=BWD_OUT,
         in_specs=[ANY] * BWD_IN,
         out_specs=[ANY] * len(BWD_OUT),
-        scratch_shapes=sems(160) + BWD_SCRATCH + BWD_WORK + Z_RING + down_scratch()
+        scratch_shapes=sems(180) + BWD_SCRATCH + BWD_WORK + Z_RING + down_scratch(80) + down_scratch(64)
         + [v for cols in PIECES for v in ring_scratch(cols)],
         compiler_params=pltpu.CompilerParams(
             collective_id=1, has_side_effects=True, vmem_limit_bytes=62 * 2**20
@@ -1355,7 +1354,7 @@
             shape(32, 4608, dtype=F32), shape(DN, 1024, dtype=F32), shape(32, 128, dtype=F32),
         ),
         in_specs=[ANY] * 5,
-        out_specs=[ANY] + [vmem] * 9,
+        out_specs=[vmem] * 10,
         scratch_shapes=[
             pltpu.VMEM((4, 32, WA), BF), pltpu.VMEM((4, 32, GU), BF), pltpu.VMEM((DN, 1024), BF),
             pltpu.VMEM((2, 128, 1024), BF), pltpu.SemaphoreType.DMA((5,)),

time: 234 us -> 200 us (0.85)
  Pallas kernels: 225 us -> 192 us
    pallas_call x1, Pallas kernels: 98.2 us -> 79.8 us  [backward(): pl.pallas_call(bwd_kernel, out_shape=BWD_OUT, in_specs=[ANY] * BWD_IN, ou...]
    pallas_call x1, Pallas kernels: 18.7 us -> 3.68 us  [finish(): pl.pallas_call(finish_kernel, out_shape=(shape(2, 128, 1024), shape(2, 12...]
where the time goes in v4:
time: 200 us
  Pallas kernels  192 us (96%)
  local copies, waits for them, and re-layouts  4.02 us (2%)
  other arithmetic  3.26 us (2%)
    pallas_call x1, Pallas kernels, forward(): pl.pallas_call(fwd_kernel, out_shape=FWD_OUT, in_specs=[ANY] * FWD_IN, ou...  109 us
    pallas_call x1, Pallas kernels, backward(): pl.pallas_call(bwd_kernel, out_shape=BWD_OUT, in_specs=[ANY] * BWD_IN, ou...  79.8 us

profile of v4, /device:TPU:0, one launch (start us, length us, event | category | flops | bytes accessed | tf_op | source)
XLA Modules:
  0.0 200.1 jit_solution(2390580291565950567)
XLA Ops:
  0.7 0.7 fusion.1
  1.4 0.5 multiply_cosine_fusion
  1.9 0.8 pad_maximum_fusion.refs_9_
  2.7 0.7 convert_element_type.22
  3.4 0.6 broadcast_in_dim.13.refs_10_
  4.0 0.8 concatenate.26
  4.8 0.5 convert_element_type.23.refs_11_
  5.3 108.7 %shard_map.237 = (bf16[4,4,2,32,3200]{4,3,2,1,0:T(8,128)(2,1)}, bf16[256,1024]{1,0:T(8,128)(2,1)}, f32[256,1024]{1,0:T(8,128)}, f32[256,512]{1,0:T(8,128)}, bf16...) custom-call(bf16[32,1024]{1,0:T(8,128)(2,1)} %refs_0_.1, ...), custom_call_target="tpu_custom_call" | custom-call | tf_op jit(solution)/shard_map/pallas_call | solution.py:976
  114.0 79.8 %shard_map.238 = (bf16[2,128,1024]{2,1,0:T(8,128)(2,1)}, bf16[2,128,1024]{2,1,0:T(8,128)(2,1)}, bf16[4,32,3200]{2,1,0:T(8,128)(2,1)}, bf16[4,32,2304]{2,1,0:T(8,128)(2,1)}, bf16[144,1024]{1,0:T(8,128)(2,1)}) custom-call(bf16[4,4,2,32,3200]{4,3,2,1,0:T(8,128)(2,1)} %get-tuple-element.45.refs_0_, bf16[256,1024]{1,0:T(8,128)(2,1)} %get-tuple-element.46.refs_1_, ...), custom_call_target="tpu_custom_call" | custom-call | tf_op jit(solution)/shard_map/pallas_call | solution.py:1307
  193.8 3.7 %shard_map.239 = (bf16[2,128,1024]{2,1,0:T(8,128)(2,1)}, f32[2,128,1024]{2,1,0:T(8,128)}, f32[32,1024]{1,0:T(8,128)}, f32[32,512]{1,0:T(8,128)}, f32[32,512]{1,0...) custom-call(bf16[2,128,1024]{2,1,0:T(8,128)(2,1)} %get-tuple-element, ...), custom_call_target="tpu_custom_call" | custom-call | tf_op jit(solution)/shard_map/pallas_call | solution.py:1349
  197.5 1.3 dynamic-slice_bitcast_fusion
  198.9 1.3 dynamic-slice_bitcast_fusion.2
  (3 shorter events, 0.0 us)

commit v5 on v4

--- a/solution.py
+++ b/solution.py
@@ -740,7 +740,7 @@
     lax.fori_loop(0, 4, last, 0)
 
 
-def feed_grads(left, right, out, tiles):
+def feed_grads(left, right, out, first, tiles):
     def step(j, _):
         cut = pl.ds(pl.multiple_of(256 * j, 256), 256)
         got = dot(left[...], flat(right[:, :, cut]), kind=BF)
@@ -748,7 +748,7 @@
         out[(slice(None),) * len(lead) + (cut,)] = got.reshape(*lead, 256)
         return 0
 
-    lax.fori_loop(0, tiles, step, 0)
+    lax.fori_loop(first, tiles, step, 0)
 
 
 FWD_SCRATCH = [
@@ -954,21 +954,23 @@
         add_into(grad_ffn.at[slot, rows], passing.at[k])
         sent.append(lk.put(grad_ffn.at[slot, rows], landing.at[rows], to))
 
-    feed_grads(turned, cots, down, 4)
+    feed_grads(turned, cots, down, 0, 4)
     saved.append(lk.keep(down, outs[12]))
     hop(0)
     hop(2)
-    feed_grads(ffn_turned, grad_both, gate_up, 9)
+    feed_grads(ffn_turned, grad_both, gate_up, 0, 4)
     hop(1)
     hop(3)
+    feed_grads(ffn_turned, grad_both, gate_up, 4, 9)
     saved.append(lk.keep(gate_up, outs[11]))
     for copy in sent:
         copy.wait_recv()
+    saved.pop(2).wait()
+    total = grad_ffn[own].astype(F32) + from_right[...].astype(F32) + from_left[...].astype(F32)
+    lin_query[...] = total
+    saved.append(lk.keep(lin_query, outs[14]))
     for copy in saved:
         copy.wait()
-    total = grad_ffn[own].astype(F32) + from_right[...].astype(F32) + from_left[...].astype(F32)
-    lin_query[...] = total
-    lk.keep(lin_query, outs[14]).wait()
     lk.flush()
 
 

time: 200 us -> 198 us (0.990)
  Pallas kernels: 192 us -> 189 us
    pallas_call x1, Pallas kernels: 109 us -> 105 us  [forward(): pl.pallas_call(fwd_kernel, out_shape=FWD_OUT, in_specs=[ANY] * FWD_IN, ou...]
where the time goes in v5:
time: 198 us; the launch traced here: 197 us
  Pallas kernels  189 us (95%)
  local copies, waits for them, and re-layouts  4.02 us (2%)
  other arithmetic  3.26 us (2%)
    pallas_call x1, Pallas kernels, forward(): pl.pallas_call(fwd_kernel, out_shape=FWD_OUT, in_specs=[ANY] * FWD_IN, ou...  105 us
    pallas_call x1, Pallas kernels, backward(): pl.pallas_call(bwd_kernel, out_shape=BWD_OUT, in_specs=[ANY] * BWD_IN, ou...  80.5 us

profile of v5, /device:TPU:0, one launch (start us, length us, event | category | flops | bytes accessed | tf_op | source)
XLA Modules:
  0.0 197.2 jit_solution(2002915818460676366)
XLA Ops:
  0.7 0.7 fusion.1
  1.4 0.5 multiply_cosine_fusion
  1.9 0.8 pad_maximum_fusion.refs_9_
  2.7 0.7 convert_element_type.22
  3.4 0.6 broadcast_in_dim.13.refs_10_
  4.0 0.8 concatenate.26
  4.8 0.5 convert_element_type.23.refs_11_
  5.3 105.1 %shard_map.237 = (bf16[4,4,2,32,3200]{4,3,2,1,0:T(8,128)(2,1)}, bf16[256,1024]{1,0:T(8,128)(2,1)}, f32[256,1024]{1,0:T(8,128)}, f32[256,512]{1,0:T(8,128)}, bf16...) custom-call(bf16[32,1024]{1,0:T(8,128)(2,1)} %refs_0_.1, ...), custom_call_target="tpu_custom_call" | custom-call | tf_op jit(solution)/shard_map/pallas_call | solution.py:978
  110.4 80.5 %shard_map.238 = (bf16[2,128,1024]{2,1,0:T(8,128)(2,1)}, bf16[2,128,1024]{2,1,0:T(8,128)(2,1)}, bf16[4,32,3200]{2,1,0:T(8,128)(2,1)}, bf16[4,32,2304]{2,1,0:T(8,128)(2,1)}, bf16[144,1024]{1,0:T(8,128)(2,1)}) custom-call(bf16[4,4,2,32,3200]{4,3,2,1,0:T(8,128)(2,1)} %get-tuple-element.45.refs_0_, bf16[256,1024]{1,0:T(8,128)(2,1)} %get-tuple-element.46.refs_1_, ...), custom_call_target="tpu_custom_call" | custom-call | tf_op jit(solution)/shard_map/pallas_call | solution.py:1309
  190.9 3.7 %shard_map.239 = (bf16[2,128,1024]{2,1,0:T(8,128)(2,1)}, f32[2,128,1024]{2,1,0:T(8,128)}, f32[32,1024]{1,0:T(8,128)}, f32[32,512]{1,0:T(8,128)}, f32[32,512]{1,0...) custom-call(bf16[2,128,1024]{2,1,0:T(8,128)(2,1)} %get-tuple-element, ...), custom_call_target="tpu_custom_call" | custom-call | tf_op jit(solution)/shard_map/pallas_call | solution.py:1351
  194.6 1.3 dynamic-slice_bitcast_fusion
  195.9 1.3 dynamic-slice_bitcast_fusion.2
  (3 shorter events, 0.0 us)
